TPU v7x, 128 devices: a whole 4x4x4 slice. The times are simulated.
128 devices in a mesh: gx: 16 (over z, x), gy: 8 (over y, core).
Axes of the slice: x: 4, y: 4, z: 4, core: 2. Of those that a mesh axis runs over, the one named last changes fastest.
Arguments:
- positions: float32 [3, 32768, 256], P(None, ('gx', 'gy')), may hold values from 0 to 1
- smooth: float32 [32768, 256], P(('gx', 'gy')), may hold values from 0.25 to 0.6
- masses: float32 [32768, 256], P(('gx', 'gy')), may hold values from 0.0002 to 0.002
- entropy: float32 [32768, 256], P(('gx', 'gy')), may hold values from 0.5 to 2
- cell_counts: int32 [32768], P(('gx', 'gy')), may hold values from 64 to 256, as said below
- cell_pairs: int32 [2, 49152], P(None, ('gx', 'gy')), may hold values from 0 to 511, as said below
- pair_count: int32 [128], P(('gx', 'gy')), may hold values from 256 to 384, as said below
- send_cells: int32 [128, 256], P(('gx', 'gy')), may hold values from -1 to 255, as said below
Outputs:
- density: float32 [32768, 256], P(('gx', 'gy'))
- acceleration: float32 [3, 32768, 256], P(None, ('gx', 'gy'))
Inputs may be any that keep to these rules, and one draw needn't show every extreme that they name: `cell_counts`: particles of a cell fill the first slots of its tile; some cell is full. `send_cells`: row r, column p * 2 + s: the local cell device r sends to device p in slot s, or -1 for an empty slot. Filled slots of each sender and receiver come first, at least one, with distinct cells; each sender fills all 2 slots for some receiver. `cell_pairs`: on each device the first 256 pairs have a ghost slot (at least 256) as second entry, naming only filled slots, and every filled slot is named; the others name two different local cells. `pair_count`: the live pairs are the first ones of each device; some device has 384.
All inputs are finite; a program needn't handle non-finite values.
Results may differ from a plain program's by a relative error of at most 0.0003.
Values sent between devices are 32-bit elements; how exact they have to be, the bound alone decides.
No kernel may reach another device: no remote copies, remote signals or barrier semaphores. Data moves between devices by JAX's collectives and lax.ppermute only.
A program may use at most 64 MiB of HBM per device.

v0:
```python
import math

import jax
import jax.numpy as jnp
from jax import lax
from jax.sharding import PartitionSpec as P

KERNEL_NORM = 21.0 / (2.0 * math.pi)


def kernel_weight(distance, smooth_len):
    scaled = distance / smooth_len
    remain = jnp.maximum(1.0 - scaled, 0.0)
    inverse = 1.0 / smooth_len
    return KERNEL_NORM * inverse * inverse * inverse * remain**4 * (1.0 + 4.0 * scaled)


def kernel_slope(distance, smooth_len):
    scaled = distance / smooth_len
    remain = jnp.maximum(1.0 - scaled, 0.0)
    inverse = 1.0 / smooth_len
    return -20.0 * KERNEL_NORM * inverse**5 * remain**3


def separations(near_pos, far_pos):
    offsets = [near_pos[axis_id][:, :, None] - far_pos[axis_id][:, None, :] for axis_id in range(3)]
    distance = jnp.sqrt(offsets[0] * offsets[0] + offsets[1] * offsets[1] + offsets[2] * offsets[2])
    return (offsets, distance)


def density_pair(near_pos, near_smooth, near_mass, far_pos, far_smooth, far_mass):
    offsets, distance = separations(near_pos, far_pos)
    rho_near = jnp.sum(
        kernel_weight(distance, near_smooth[:, :, None]) * far_mass[:, None, :], axis=2
    )
    rho_far = jnp.sum(
        kernel_weight(distance, far_smooth[:, None, :]) * near_mass[:, :, None], axis=1
    )
    return (rho_near, rho_far)


def force_pair(
    near_pos, near_smooth, near_mass, near_factor, far_pos, far_smooth, far_mass, far_factor
):
    offsets, distance = separations(near_pos, far_pos)
    coupling = near_factor[:, :, None] * kernel_slope(distance, near_smooth[:, :, None])
    coupling = coupling + far_factor[:, None, :] * kernel_slope(distance, far_smooth[:, None, :])
    near_weighted = coupling * far_mass[:, None, :]
    far_weighted = coupling * near_mass[:, :, None]
    acc_near = jnp.stack(
        [-jnp.sum(near_weighted * offsets[axis_id], axis=2) for axis_id in range(3)]
    )
    acc_far = jnp.stack([jnp.sum(far_weighted * offsets[axis_id], axis=1) for axis_id in range(3)])
    return (acc_near, acc_far)


def trade_fields(payload):
    return lax.all_to_all(payload, ("gx", "gy"), split_axis=1, concat_axis=1, tiled=True)


def trade_density(payload):
    return lax.all_to_all(payload, ("gx", "gy"), split_axis=1, concat_axis=1, tiled=True)


def trade_factor(payload):
    return lax.all_to_all(payload, ("gx", "gy"), split_axis=1, concat_axis=1, tiled=True)


def trade_accel(payload):
    return lax.all_to_all(payload, ("gx", "gy"), split_axis=1, concat_axis=1, tiled=True)


def local(positions, smooth, masses, entropy, cell_counts, cell_pairs, pair_count, send_cells):
    num_cells = positions.shape[1]
    tile_len = positions.shape[2]
    group_len = 16
    usable = (
        lax.broadcasted_iota(jnp.int32, (num_cells, tile_len), 1) < cell_counts[:, None]
    ).astype(jnp.float32)
    live_mass = masses * usable
    targets = send_cells[0]
    filled = (targets >= 0).astype(jnp.float32)
    clipped = jnp.maximum(targets, 0)
    local_fields = jnp.concatenate([positions, smooth[None], live_mass[None]], axis=0)
    outgoing = jnp.take(local_fields, clipped, axis=1) * filled[None, :, None]
    ghosts = trade_fields(outgoing)
    num_ghosts = ghosts.shape[1]
    all_fields = jnp.concatenate([local_fields, ghosts], axis=1)
    num_pairs = cell_pairs.shape[1]
    turns = num_pairs // group_len
    living = (jnp.arange(num_pairs, dtype=jnp.int32) < pair_count[0]).astype(jnp.float32)
    pair_items = (
        cell_pairs[0].reshape(turns, group_len),
        cell_pairs[1].reshape(turns, group_len),
        living.reshape(turns, group_len),
    )
    group_ids = jnp.arange(num_cells // group_len, dtype=jnp.int32)

    def self_density(group_index):
        piece = lax.dynamic_slice_in_dim(local_fields, group_index * group_len, group_len, 1)
        return density_pair(piece[0:3], piece[3], piece[4], piece[0:3], piece[3], piece[4])[0]

    def density_step(running, entry_item):
        first_ids, second_ids, alive_now = entry_item
        near_side = jnp.take(all_fields, first_ids, axis=1)
        far_side = jnp.take(all_fields, second_ids, axis=1)
        rho_near, rho_far = density_pair(
            near_side[0:3],
            near_side[3],
            near_side[4] * alive_now[:, None],
            far_side[0:3],
            far_side[3],
            far_side[4] * alive_now[:, None],
        )
        return (running.at[first_ids].add(rho_near).at[second_ids].add(rho_far), None)

    self_rho = lax.map(self_density, group_ids).reshape(num_cells, tile_len)
    pair_rho, _ = lax.scan(
        density_step, jnp.zeros((num_cells + num_ghosts, tile_len), jnp.float32), pair_items
    )
    returned_rho = trade_density(pair_rho[num_cells:][None])[0]
    selector = (
        targets[None, :] == lax.broadcasted_iota(jnp.int32, (num_cells, num_ghosts), 0)
    ).astype(jnp.float32)
    credited = jnp.dot(
        selector, returned_rho, precision=lax.Precision.HIGHEST, preferred_element_type=jnp.float32
    )
    density = (self_rho + pair_rho[:num_cells] + credited) * usable
    clipped_rho = jnp.where(usable > 0, density, 1.0)
    factor = jnp.where(usable > 0, entropy * clipped_rho ** (-1.0 / 3.0), 0.0)
    outgoing_factor = jnp.take(factor, clipped, axis=0) * filled[:, None]
    ghost_factor = trade_factor(outgoing_factor[None])[0]
    all_factor = jnp.concatenate([factor, ghost_factor], axis=0)

    def self_force(group_index):
        piece = lax.dynamic_slice_in_dim(local_fields, group_index * group_len, group_len, 1)
        piece_factor = lax.dynamic_slice_in_dim(factor, group_index * group_len, group_len, 0)
        return force_pair(
            piece[0:3],
            piece[3],
            piece[4],
            piece_factor,
            piece[0:3],
            piece[3],
            piece[4],
            piece_factor,
        )[0]

    def force_step(running, entry_item):
        first_ids, second_ids, alive_now = entry_item
        near_side = jnp.take(all_fields, first_ids, axis=1)
        far_side = jnp.take(all_fields, second_ids, axis=1)
        acc_near, acc_far = force_pair(
            near_side[0:3],
            near_side[3],
            near_side[4] * alive_now[:, None],
            jnp.take(all_factor, first_ids, axis=0),
            far_side[0:3],
            far_side[3],
            far_side[4] * alive_now[:, None],
            jnp.take(all_factor, second_ids, axis=0),
        )
        return (running.at[:, first_ids].add(acc_near).at[:, second_ids].add(acc_far), None)

    self_acc = jnp.moveaxis(lax.map(self_force, group_ids), 1, 0).reshape(3, num_cells, tile_len)
    pair_acc, _ = lax.scan(
        force_step, jnp.zeros((3, num_cells + num_ghosts, tile_len), jnp.float32), pair_items
    )
    returned_acc = trade_accel(pair_acc[:, num_cells:])
    credited_acc = jnp.einsum(
        "cg,kgp->kcp",
        selector,
        returned_acc,
        precision=lax.Precision.HIGHEST,
        preferred_element_type=jnp.float32,
    )
    acceleration = (self_acc + pair_acc[:, :num_cells] + credited_acc) * usable[None]
    return (density, acceleration)


def solution(mesh):
    in_specs = (
        P(None, ("gx", "gy"), None),
        P(("gx", "gy"), None),
        P(("gx", "gy"), None),
        P(("gx", "gy"), None),
        P(("gx", "gy")),
        P(None, ("gx", "gy")),
        P(("gx", "gy")),
        P(("gx", "gy"), None),
    )
    out_specs = (P(("gx", "gy"), None), P(None, ("gx", "gy"), None))
    return jax.shard_map(local, mesh=mesh, in_specs=in_specs, out_specs=out_specs, check_vma=False)
```

profile of v0, /device:TPU:1, one launch (start us, length us, event | category | flops | bytes accessed | tf_op | source)
XLA Modules:
  0.0 1216.0 jit_solution(6248290470804732825)
XLA Ops:
  13.1 12.0 all-to-all-start
  26.5 133.3 %while.40 = (s32[]{:T(128)}, f32[16,16,256]{2,1,0:T(8,128)}, s32[16]{0:T(128)S(1)}, f32[5,256,256]{2,1,0:T(8,128)}, s32[]{:T(128)}, /*index=5*/s32[1]{0:T(128)},...) while((s32[]{:T(128)}, f32[16,16,256]{2,1,0:T(8,128)}, s32[16]{0:T(128)S(1)}, ...), condition=%wide.region_2.3_spmd, body=%wide.region_0.0_spmd.sunk | while | flops 19935240 | bytes 327939 | solution.py:117
  165.2 356.4 %while.41 = (s32[]{:T(128)}, f32[512,256]{1,0:T(8,128)S(1)}, s32[24,16]{1,0:T(8,128)S(1)}, f32[5,512,256]{2,0,1:T(8,128)}, s32[24,16]{1,0:T(8,128)S(1)}, /*index=5*/f32[24,16]{1,0:T(8,128)S(1)}, s32[]{:T(128)}) while((s32[]{:T(128)}, f32[512,256]{1,0:T(8,128)S(1)}, s32[24,16]{1,0:T(8,128)S(1)}, f32[5,512,256]{2,0,1:T(8,128)}, ...), condition=%wide.region_8.10_spmd, body=%wide.region_3.9_spmd.sunk | while | flops 31541536 | bytes 1549537 | solution.py:118
  521.9 20.7 %all_to_all.20 = f32[1,256,256]{2,0,1:T(1,128)S(1)} all-to-all(f32[1,256,256]{2,0,1:T(1,128)S(1)} %broadcast_in_dim.99), channel_id=1, replica_groups=mesh['gx'=16,'gy'=8] {'gx','gy'}, dimensions={1} | all-to-all | bytes 524288 | tf_op jit(solution)/shard_map/all_to_all | solution.py:62
  551.2 10.1 all-to-all-done.2
  561.7 462.4 %while.43 = (s32[]{:T(128)}, f32[3,512,256]{2,0,1:T(4,128)S(1)}, s32[24,16]{1,0:T(8,128)S(1)}, f32[512,256]{1,0:T(8,128)S(1)}, f32[5,512,256]{2,0,1:T(8,128)}, /...) while((s32[]{:T(128)}, f32[3,512,256]{2,0,1:T(4,128)S(1)}, s32[24,16]{1,0:T(8,128)S(1)}, ...), condition=%wide.region_23.26_spmd, body=%wide.region_14.25_spmd.sunk | while | flops 38959392 | bytes 2467209 | solution.py:166
  588.2 9.6 fusion.78
  607.5 9.6 fusion.78
  626.7 9.6 fusion.78
  646.0 9.6 fusion.78
  665.3 9.6 fusion.78
  684.5 9.6 fusion.78
  703.8 9.6 fusion.78
  723.0 9.6 fusion.78
  742.3 9.6 fusion.78
  761.6 9.6 fusion.78
  780.8 9.6 fusion.78
  800.1 9.6 fusion.78
  819.4 9.6 fusion.78
  838.6 9.6 fusion.78
  877.2 9.6 fusion.78
  896.4 9.6 fusion.78
  915.7 9.6 fusion.78
  1029.5 178.9 %while.42 = (s32[]{:T(128)}, f32[16,3,16,256]{3,2,0,1:T(8,128)}, s32[16]{0:T(128)S(1)}, f32[256,256]{1,0:T(8,128)S(1)}, f32[5,256,256]{2,1,0:T(8,128)}, /*index=...) while((s32[]{:T(128)}, f32[16,3,16,256]{3,2,0,1:T(8,128)}, ...), condition=%wide.region_13.15_spmd, body=%wide.region_9.14_spmd.sunk | while | flops 31502344 | bytes 573707 | solution.py:165
  (1470 shorter events, 980.7 us)
Async XLA Ops:
  3.1 3.2 copy-start
  13.1 147.6 %all-to-all-start = ((f32[5,256,256]{2,0,1:T(8,128)}), f32[5,256,256]{2,0,1:T(8,128)}, u32[]{:S(2)}, u32[]{:S(2)}) async-start(f32[5,256,256]{2,0,1:T(8,128)} %multiply_bitcast_fusion), calls=%async_computation | async-start | bytes 4194304 | tf_op jit(solution)/shard_map/all_to_all | solution.py:58
  26.5 133.3 %copy-start.6 = (s32[2,384]{1,0:T(2,128)S(1)}, s32[2,384]{1,0:T(2,128)}, u32[]{:S(2)}) copy-start(s32[2,384]{1,0:T(2,128)} %param.25) | copy-start | bytes 9220
  26.5 134.2 %copy-start.1 = (f32[1,256,256]{2,0,1:T(1,128)S(1)}, f32[1,256,256]{2,0,1:T(1,128)}, u32[]{:S(2)}) copy-start(f32[1,256,256]{2,0,1:T(1,128)} %copy-done) | copy-start | bytes 786436
  165.1 356.5 %copy-start.3 = (f32[16,16,256]{2,1,0:T(8,128)S(1)}, f32[16,16,256]{2,1,0:T(8,128)}, u32[]{:S(2)}) copy-start(f32[16,16,256]{2,1,0:T(8,128)} %get-tuple-element.122) | copy-start | bytes 786436
  165.1 377.4 %copy-start.2 = (f32[256,256]{1,0:T(8,128)S(1)}, f32[256,256]{1,0:T(8,128)}, u32[]{:S(2)}) copy-start(f32[256,256]{1,0:T(8,128)} %param.23) | copy-start | bytes 786436
  165.2 377.4 %copy-start.4 = (s32[1,256]{1,0:T(1,128)S(1)}, s32[1,256]{1,0:T(1,128)}, u32[]{:S(2)}) copy-start(s32[1,256]{1,0:T(1,128)} %param.27) | copy-start | bytes 3076
  165.2 377.4 %copy-start.5 = (s32[256]{0:T(256)S(1)}, s32[256]{0:T(256)}, u32[]{:S(2)}) copy-start(s32[256]{0:T(256)} %param.24) | copy-start | bytes 3076
  545.9 15.4 %all-to-all-start.2 = ((f32[1,256,256]{2,0,1:T(1,128)}), f32[1,256,256]{2,0,1:T(1,128)S(1)}, u32[]{:S(2)}, u32[]{:S(2)}) async-start(f32[1,256,256]{2,0,1:T(1,128)} %copy.55), calls=%async_computation.2 | async-start | bytes 524288 | tf_op jit(solution)/shard_map/all_to_all | solution.py:66
  1025.2 187.4 %all-to-all-start.3 = ((f32[3,256,256]{2,0,1:T(4,128)}), f32[3,256,256]{2,0,1:T(4,128)S(1)}, u32[]{:S(2)}, u32[]{:S(2)}) async-start(f32[3,256,256]{2,0,1:T(4,128)} %slice.146), calls=%async_computation.3 | async-start | bytes 2097152 | tf_op jit(solution)/shard_map/all_to_all | solution.py:70
where the time goes:
time: 1220 us
  other arithmetic  764 us (63%)
  local copies, waits for them, and re-layouts  368 us (30%)
  loops' own time  28 us (2%)
  blocking collectives  20.7 us (2%)
  starting transfers between devices  20.6 us (2%)
    reduce_sum x24, other arithmetic, force_pair(): jnp.sum(far_weighted * offsets[axis_id], axis=1)  230 us
    reduce_sum x24, other arithmetic, density_pair(): jnp.sum(kernel_weight(distance, far_smooth[:, None, :]) * near_mass[:, :,...  169 us
    reduce_sum x16, other arithmetic, force_pair(): jnp.sum(near_weighted * offsets[axis_id], axis=2)  125 us
    reduce_sum x16, other arithmetic, density_pair(): jnp.sum(kernel_weight(distance, near_smooth[:, :, None]) * far_mass[:, No...  79.7 us
    gather x24, local copies, waits for them, and re-layouts, density_step(): far_side = jnp.take(all_fields, second_ids, axis=1)  66 us
    gather x24, local copies, waits for them, and re-layouts, force_step(): near_side = jnp.take(all_fields, first_ids, axis=1)  65.9 us
    gather x24, local copies, waits for them, and re-layouts, density_step(): near_side = jnp.take(all_fields, first_ids, axis=1)  65.9 us
    gather x24, local copies, waits for them, and re-layouts, force_step(): far_side = jnp.take(all_fields, second_ids, axis=1)  65.9 us
  transfers between devices with their start and end apart: 3, of which 1 were waited for; matrix products, arithmetic and copies ran while one was open for 25% of the time, Pallas kernels for 0%

commit v1 on v0

v1 whole, which is shorter than its diff:
```python
import functools
import math

import jax
import jax.numpy as jnp
from jax import lax
from jax.experimental import pallas as pl
from jax.experimental.pallas import tpu as pltpu
from jax.sharding import PartitionSpec as P

KERNEL_NORM = 21.0 / (2.0 * math.pi)
AXES = ("gx", "gy")
LANES = 128
TILE = 256
ROWS = 64
CHUNKS = TILE // ROWS
TINY = 1e-30
F32 = jnp.float32
BF16 = jnp.bfloat16

ROW_NORM, ROW_ONE, ROW_H, ROW_MASS, ROW_G = 3, 4, 5, 6, 7

NN = (((1,), (0,)), ((), ()))
TN = (((0,), (0,)), ((), ()))
NT = (((1,), (1,)), ((), ()))


def mxu(a, b, dims):
    return lax.dot_general(a, b, dims, preferred_element_type=F32)


def pieces3(x):
    a = x.astype(BF16).astype(F32)
    r = x - a
    b = r.astype(BF16).astype(F32)
    c = r - b
    return a, b, c


def left_stack(x):
    a, b, c = pieces3(x)
    return jnp.concatenate([a, a, b, b, a, c], axis=0).astype(BF16)


def right_stack(x):
    a, b, c = pieces3(x)
    return jnp.concatenate([a, b, a, b, c, a], axis=0).astype(BF16)


def hi_lo_rows(x):
    hi = x.astype(BF16).astype(F32)
    return jnp.concatenate([hi, x - hi], axis=0).astype(BF16)


def twice(x):
    return jnp.concatenate([x, x], axis=1)


def row_fields(f_ref, i):
    block = f_ref[i >> 1]
    return pltpu.roll(block, (i & 1) * ROWS, axis=1)[:, :ROWS]


def lane_fields(f_ref, j):
    return jnp.concatenate([f_ref[2 * j], f_ref[2 * j + 1]], axis=1)


def distances(f_ref, pick, i, j):
    left = left_stack(row_fields(f_ref, i))
    lanes = lane_fields(f_ref, j)
    row = lax.broadcasted_iota(jnp.int32, (8, TILE), 0)
    norm = lanes[ROW_NORM : ROW_NORM + 1, :]
    right = jnp.where(row < 3, -2.0 * lanes, jnp.where(row == ROW_ONE, norm, jnp.where(row == ROW_NORM, 1.0, 0.0)))
    return mxu(left, right_stack(right), TN), mxu(left, pick, TN)


def lane_row(f_ref, j, which):
    return jnp.concatenate(
        [f_ref[2 * j, which : which + 1, :], f_ref[2 * j + 1, which : which + 1, :]], axis=1
    )


def fold_rows(x):
    total = x[0:8]
    for k in range(1, x.shape[0] // 8):
        total = total + x[8 * k : 8 * k + 8]
    return total


def density_self_values(parts, f_ref, i, j):
    squared, column = parts
    squared = jnp.maximum(squared, TINY)
    dist = squared * lax.rsqrt(squared)
    h = lane_row(f_ref, j, ROW_H)
    t = jnp.maximum(h - dist, 0.0)
    t = t * t
    return fold_rows(t * t * (h + 4.0 * dist) * twice(column))


def density_pair_values(parts, f_ref, i, j):
    squared, column = parts
    squared = jnp.maximum(squared, TINY)
    dist = squared * lax.rsqrt(squared)
    four = 4.0 * dist
    h_row, m_row = twice(column[:, :LANES]), twice(column[:, LANES:])
    h, m = lane_row(f_ref, j, ROW_H), lane_row(f_ref, j, ROW_MASS)
    t = jnp.maximum(h_row - dist, 0.0)
    t = t * t
    near = t * t * (h_row + four) * m
    s = jnp.maximum(h - dist, 0.0)
    s = s * s
    far = s * s * (h + four) * m_row
    return near[:, :LANES] + near[:, LANES:], fold_rows(far)


def density_self_store(values, f_ref, out, i, j):
    out[2 * j] += values[:, :LANES]
    out[2 * j + 1] += values[:, LANES:]


def density_pair_store(values, f_ref, out, col, i, j):
    near, far = values
    out[2 * j] += far[:, :LANES]
    out[2 * j + 1] += far[:, LANES:]
    lane = lax.broadcasted_iota(jnp.int32, (ROWS, LANES), 1)
    total = jnp.sum(near, axis=1, keepdims=True)
    col[i >> 7] += jnp.where(lane == (i & 127), total, 0.0)


def force_values(parts, f_ref, i, j):
    squared, column = parts
    squared = jnp.maximum(squared, TINY)
    dist = squared * lax.rsqrt(squared)
    h_row, g_row = twice(column[:, :LANES]), twice(column[:, LANES:])
    h, g = lane_row(f_ref, j, ROW_H), lane_row(f_ref, j, ROW_G)
    a = jnp.maximum(h_row - dist, 0.0)
    b = jnp.maximum(h - dist, 0.0)
    coupling = g_row * (a * a * a) + g * (b * b * b)
    hi = coupling.astype(BF16)
    lo = (coupling - hi.astype(F32)).astype(BF16)
    return hi, lo


def force_far_store(values, f_ref, out, i, j):
    hi, lo = values
    rows = row_fields(f_ref, i)
    moments = hi_lo_rows(rows * rows[ROW_MASS : ROW_MASS + 1, :])
    far = fold_rows(mxu(moments, hi, NN) + mxu(moments, lo, NN))
    out[2 * j] += far[:, :LANES]
    out[2 * j + 1] += far[:, LANES:]


def force_pair_store(values, f_ref, out, i, j):
    hi, lo = values
    force_far_store(values, f_ref, out, i, j)
    lanes = lane_fields(f_ref, j)
    moments = hi_lo_rows(lanes * lanes[ROW_MASS : ROW_MASS + 1, :])
    near = twice(fold_rows(mxu(moments, hi, NT) + mxu(moments, lo, NT)))
    lane = lax.broadcasted_iota(jnp.int32, (8, LANES), 1)
    out[i >> 1] += jnp.where((lane >> 6) == (i & 1), near, 0.0)


def sweep(unroll, lead, lag, count, units, stage_a, stage_b, stage_c):
    def body(step, carry):
        ids = []
        for k in range(unroll):
            code = units[step * unroll + k]
            ids.append((code >> 16, code & 0xFFFF))
        parts, values = {}, {}
        for k in range(-lead, unroll + lag):
            if 0 <= k + lead < unroll:
                parts[k + lead] = stage_a(*ids[k + lead])
            if 0 <= k < unroll:
                values[k] = stage_b(parts.pop(k), *ids[k])
            if 0 <= k - lag < unroll:
                stage_c(values.pop(k - lag), *ids[k - lag])
        return carry

    lax.fori_loop(0, count, body, 0)


def density_self_kernel(unroll, count, units, f_ref, pick, out):
    out[...] = jnp.zeros_like(out)
    sweep(
        unroll, 2, 1, count[0], units,
        lambda i, j: distances(f_ref, pick[:, LANES:], i, j),
        lambda p, i, j: density_self_values(p, f_ref, i, j),
        lambda v, i, j: density_self_store(v, f_ref, out, i, j),
    )


def density_pair_kernel(unroll, count, units, f_ref, pick, out, col):
    out[...] = jnp.zeros_like(out)
    col[...] = jnp.zeros_like(col)
    sweep(
        unroll, 3, 2, count[0], units,
        lambda i, j: distances(f_ref, pick[...], i, j),
        lambda p, i, j: density_pair_values(p, f_ref, i, j),
        lambda v, i, j: density_pair_store(v, f_ref, out, col, i, j),
    )


def force_kernel(unroll, both, count, units, f_ref, pick, out):
    out[...] = jnp.zeros_like(out)
    store = force_pair_store if both else force_far_store
    sweep(
        unroll, 3, 3, count[0], units,
        lambda i, j: distances(f_ref, pick[...], i, j),
        lambda p, i, j: force_values(p, f_ref, i, j),
        lambda v, i, j: store(v, f_ref, out, i, j),
    )


def run_kernel(body, name, count, units, fields, pick, with_col, est_units):
    smem = pl.BlockSpec(memory_space=pltpu.SMEM)
    vmem = pl.BlockSpec(memory_space=pltpu.VMEM)
    blocks = fields.shape[0]
    shapes = [jax.ShapeDtypeStruct((blocks, 8, LANES), F32)]
    if with_col:
        groups = (2 * blocks + LANES - 1) // LANES
        shapes.append(jax.ShapeDtypeStruct((groups, ROWS, LANES), F32))
    out = pl.pallas_call(
        body,
        out_shape=shapes,
        in_specs=[smem, smem, vmem, vmem],
        out_specs=[vmem] * len(shapes),
        name=name,
        compiler_params=pltpu.CompilerParams(vmem_limit_bytes=40 * 1024 * 1024),
        cost_estimate=pl.CostEstimate(
            flops=est_units * ROWS * TILE * 2000, bytes_accessed=2 * fields.size * 4, transcendentals=0
        ),
    )(count, units, fields, pick)
    return out


def pick_matrix(second):
    k = lax.broadcasted_iota(jnp.int32, (48, TILE), 0)
    lane = lax.broadcasted_iota(jnp.int32, (48, TILE), 1)
    group, row = k // 8, k % 8
    used = (group == 0) | (group == 2) | (group == 5)
    return (used & (row == jnp.where(lane < LANES, ROW_H, second))).astype(BF16)


def compact(valid, code, spare, unroll):
    num = valid.shape[0]
    flags = valid.astype(jnp.int32)
    ids = jnp.arange(num, dtype=jnp.int32)
    rank = jnp.sum(jnp.where(ids[None, :] < ids[:, None], flags[None, :], 0), axis=1)
    total = jnp.sum(flags)
    hit = (rank[None, :] == ids[:, None]) & valid[None, :]
    listed = jnp.sum(jnp.where(hit, code[None, :], 0), axis=1)
    listed = jnp.where(ids < total, listed, spare)
    return listed.astype(jnp.int32), ((total + unroll - 1) // unroll).reshape(1).astype(jnp.int32)


def look_up(table, ids):
    slots = jnp.arange(table.shape[0], dtype=jnp.int32)
    return jnp.sum(jnp.where(ids[:, None] == slots[None, :], table[None, :], 0), axis=1)


def pair_units(first, second, live, counts, unroll):
    num_cells = counts.shape[0]
    n_first, n_second = look_up(counts, first), look_up(counts, second)
    swap = n_second < n_first
    rows = jnp.where(swap, second, first)
    lanes = jnp.where(swap, first, second)
    chunks = (jnp.minimum(n_first, n_second) + ROWS - 1) // ROWS
    step = jnp.arange(CHUNKS, dtype=jnp.int32)
    valid = (step[None, :] < chunks[:, None]) & live[:, None]
    code = ((rows[:, None] * CHUNKS + step[None, :]) << 16) | lanes[:, None]
    spare = ((num_cells * CHUNKS) << 16) | num_cells
    return compact(valid.reshape(-1), code.reshape(-1), spare, unroll)


def to_blocks(fields):
    cells = fields.shape[0]
    blocks = fields.reshape(cells, 8, 2, LANES).transpose(0, 2, 1, 3).reshape(2 * cells, 8, LANES)
    return jnp.concatenate([blocks, jnp.zeros((2, 8, LANES), F32)], axis=0)


def spread(x):
    c = x[0:3] - 0.5
    norm = c[0] * c[0] + c[1] * c[1] + c[2] * c[2]
    return jnp.stack([c[0], c[1], c[2], norm, jnp.ones_like(norm), x[3], x[4], jnp.zeros_like(norm)], axis=1)


def with_factor(fields, g):
    return jnp.concatenate([fields[:, :7], g[:, None, :]], axis=1)


def from_blocks(blocks, cells):
    return blocks[: 2 * cells].reshape(cells, 2, 8, LANES).transpose(2, 0, 1, 3).reshape(8, cells, TILE)


def from_columns(col, cells):
    return col.transpose(0, 2, 1).reshape(-1, TILE)[:cells]


def trade(payload):
    return lax.all_to_all(payload, AXES, split_axis=1, concat_axis=1, tiled=True)


def local(positions, smooth, masses, entropy, cell_counts, cell_pairs, pair_count, send_cells):
    cells, tile = smooth.shape
    num_pairs = cell_pairs.shape[1]
    unroll = 16
    usable = (lax.broadcasted_iota(jnp.int32, (cells, tile), 1) < cell_counts[:, None]).astype(F32)
    live_mass = masses * usable
    targets = send_cells[0]
    clipped = jnp.maximum(targets, 0)
    local_raw = jnp.concatenate([positions, smooth[None], live_mass[None]], axis=0)
    ghosts_raw = trade(jnp.take(local_raw, clipped, axis=1))
    slots = ghosts_raw.shape[1]

    own = spread(local_raw)
    own_blocks = to_blocks(own)
    pick_m, pick_g = pick_matrix(ROW_MASS), pick_matrix(ROW_G)

    step = jnp.arange(CHUNKS, dtype=jnp.int32)
    ids = jnp.arange(cells, dtype=jnp.int32)
    self_valid = step[None, :] < ((cell_counts + ROWS - 1) // ROWS)[:, None]
    self_code = ((ids[:, None] * CHUNKS + step[None, :]) << 16) | ids[:, None]
    self_units, self_count = compact(
        self_valid.reshape(-1), self_code.reshape(-1), ((cells * CHUNKS) << 16) | cells, unroll
    )
    live_pair = jnp.arange(num_pairs, dtype=jnp.int32) < pair_count[0]
    first, second = cell_pairs[0], cell_pairs[1]
    inner_units, inner_count = pair_units(first[slots:], second[slots:], live_pair[slots:], cell_counts, unroll)

    (self_rho,) = run_kernel(
        functools.partial(density_self_kernel, unroll), "density_self", self_count, self_units, own_blocks, pick_m, False, 768
    )

    ghost_counts = jnp.sum((ghosts_raw[4] > 0).astype(jnp.int32), axis=1)
    all_counts = jnp.concatenate([cell_counts, ghost_counts])
    outer_units, outer_count = pair_units(first[:slots], second[:slots], live_pair[:slots], all_counts, unroll)
    ghosts = spread(ghosts_raw)
    everything = jnp.concatenate([own, ghosts], axis=0)
    all_blocks = to_blocks(everything)

    outer_rho, outer_col = run_kernel(
        functools.partial(density_pair_kernel, unroll), "density_outer", outer_count, outer_units, all_blocks, pick_m, True, 640
    )
    outer_total = jnp.sum(from_blocks(outer_rho, cells + slots), axis=0) + from_columns(outer_col, cells + slots)
    scale = KERNEL_NORM / everything[:, ROW_H] ** 8
    outer_total = outer_total * scale
    returned_rho = trade(outer_total[None, cells:])[0]

    inner_rho, inner_col = run_kernel(
        functools.partial(density_pair_kernel, unroll), "density_inner", inner_count, inner_units, own_blocks, pick_m, True, 320
    )
    inner_total = jnp.sum(from_blocks(self_rho + inner_rho, cells), axis=0) + from_columns(inner_col, cells)
    selector = (targets[None, :] == lax.broadcasted_iota(jnp.int32, (cells, slots), 0)).astype(F32)
    credited = jnp.dot(selector, returned_rho, precision=lax.Precision.HIGHEST, preferred_element_type=F32)
    density = (inner_total * scale[:cells] + outer_total[:cells] + credited) * usable
    clipped_rho = jnp.where(usable > 0, density, 1.0)
    factor = jnp.where(usable > 0, entropy * clipped_rho ** (-1.0 / 3.0), 0.0)

    ghost_factor = trade(jnp.take(factor, clipped, axis=0)[None])[0]

    own_g = 20.0 * scale[:cells] * factor
    own_blocks_g = to_blocks(with_factor(own, own_g))
    (self_acc,) = run_kernel(
        functools.partial(force_kernel, unroll, False), "force_self", self_count, self_units, own_blocks_g, pick_g, False, 768
    )
    ghost_g = 20.0 * scale[cells:] * ghost_factor
    all_blocks_g = to_blocks(with_factor(everything, jnp.concatenate([own_g, ghost_g], axis=0)))
    (outer_acc,) = run_kernel(
        functools.partial(force_kernel, unroll, True), "force_outer", outer_count, outer_units, all_blocks_g, pick_g, False, 640
    )
    outer_acc = from_blocks(outer_acc, cells + slots)
    ghost_acc = ghosts[:, 0:3].transpose(1, 0, 2) * outer_acc[ROW_ONE, cells:] - outer_acc[0:3, cells:]
    returned_acc = trade(ghost_acc)

    (inner_acc,) = run_kernel(
        functools.partial(force_kernel, unroll, True), "force_inner", inner_count, inner_units, own_blocks_g, pick_g, False, 320
    )
    moments = from_blocks(self_acc + inner_acc, cells) + outer_acc[:, :cells]
    credited_acc = jnp.einsum(
        "cg,kgp->kcp", selector, returned_acc, precision=lax.Precision.HIGHEST, preferred_element_type=F32
    )
    own_acc = own[:, 0:3].transpose(1, 0, 2) * moments[ROW_ONE] - moments[0:3]
    acceleration = (own_acc + credited_acc) * usable[None]
    return (density, acceleration)


def solution(mesh):
    in_specs = (
        P(None, AXES, None),
        P(AXES, None),
        P(AXES, None),
        P(AXES, None),
        P(AXES),
        P(None, AXES),
        P(AXES),
        P(AXES, None),
    )
    out_specs = (P(AXES, None), P(None, AXES, None))
    return jax.shard_map(local, mesh=mesh, in_specs=in_specs, out_specs=out_specs, check_vma=False)
```

time: 1220 us -> 422 us (0.35)
  other arithmetic: 764 us -> 30.3 us
  local copies, waits for them, and re-layouts: 368 us -> 64.6 us
  Pallas kernels: 0 us -> 240 us
  loops' own time: 28 us -> 0 us
  starting transfers between devices: 20.6 us -> 45.5 us
  blocking collectives: 20.7 us -> 0 us
  waiting for transfers between devices: 10.1 us -> 27.1 us
    reduce_sum x80 -> x12, other arithmetic: 604 us -> 6.64 us  [the longest x3 2.09 us: compact(): listed = jnp.sum(jnp.where(hit, code[None, :], 0), axis=1)]
    gather x146 -> x2, local copies, waits for them, and re-layouts: 295 us -> 3.31 us  [the longest x1 2.35 us: local(): ghosts_raw = trade(jnp.take(local_raw, clipped, axis=1))]
    pallas_call x0 -> x6, Pallas kernels: none -> 240 us  [run_kernel(): pl.pallas_call(body, out_shape=shapes, in_specs=[smem, smem, vmem, vmem],...]
    scatter-add x96 -> x0, other arithmetic: 97 us -> none  [the longest x48 53.6 us: force_step(): running.at[:, first_ids].add(acc_near).at[:, second_ids].add(acc_far)]
    mul x130 -> x5, other arithmetic: 31.1 us -> 2.27 us  [the longest x1 2.2 us: local(): outer_total = outer_total * scale]
    another operation x4 -> x0, loops' own time: 28 us -> none  [the longest x1 10.2 us: local(): self_rho = lax.map(self_density, group_ids).reshape(num_cells, tile_len)]
    all_to_all x3 -> x4, starting transfers between devices: 20.6 us -> 45.5 us  [trade(): lax.all_to_all(payload, AXES, split_axis=1, concat_axis=1, tiled=True)]
    sub x80 -> x1, local copies, waits for them, and re-layouts: 25.4 us -> 1.51 us  [local(): ghosts[:, 0:3].transpose(1, 0, 2) * outer_acc[ROW_ONE, cells:]]
  transfers between devices with their start and end apart: 3 -> 4, of which waited for: 1 -> 2; matrix products, arithmetic and copies ran while one was open for 25% -> 6% of each run, Pallas kernels for 0% -> 33%
where the time goes in v1:
time: 422 us; the launch traced here: 418 us
  Pallas kernels  240 us (57%)
  local copies, waits for them, and re-layouts  64.6 us (15%)
  starting transfers between devices  45.5 us (11%)
  other arithmetic  30.3 us (7%)
  waiting for transfers between devices  27.1 us (6%)
  matrix products  5.48 us (1%)
  between operations  4.3 us (1%)
    pallas_call x6, Pallas kernels, run_kernel(): pl.pallas_call(body, out_shape=shapes, in_specs=[smem, smem, vmem, vmem],...  240 us
    all_to_all x4, starting transfers between devices, trade(): lax.all_to_all(payload, AXES, split_axis=1, concat_axis=1, tiled=True)  45.5 us
    all_to_all x4, waiting for transfers between devices, trade(): lax.all_to_all(payload, AXES, split_axis=1, concat_axis=1, tiled=True)  27.1 us
    another operation x5, local copies, waits for them, and re-layouts  10.3 us
    reshape x2, local copies, waits for them, and re-layouts, from_blocks(): blocks[:2 * cells].reshape(cells, 2, 8, LANES).transpose(2, 0, 1, 3)  9.44 us
  transfers between devices with their start and end apart: 4, of which 2 were waited for; matrix products, arithmetic and copies ran while one was open for 6% of the time, Pallas kernels for 33%

profile of v1, /device:TPU:1, one launch (start us, length us, event | category | flops | bytes accessed | tf_op | source)
XLA Modules:
  0.0 417.6 jit_solution(1080572454124623319)
XLA Ops:
  6.8 3.3 select_bitcast_fusion
  10.1 12.3 %all-to-all-start = ((f32[5,256,256]{2,0,1:T(8,128)}), f32[5,256,256]{2,0,1:T(8,128)}, u32[]{:S(2)}, u32[]{:S(2)}) async-start(f32[5,256,256]{2,0,1:T(8,128)} %select_bitcast_fusion), calls=%async_computation | async-start | bytes 4194304 | tf_op jit(solution)/shard_map/all_to_all | solution.py:300
  33.5 18.9 %all-to-all-done = f32[5,256,256]{2,0,1:T(8,128)} async-done(((f32[5,256,256]{2,0,1:T(8,128)}), f32[5,256,256]{2,0,1:T(8,128)}, u32[]{:S(2)}, u32[]{:S(2)}) %all-to-all-start) | async-done | bytes 1310752 | tf_op jit(solution)/shard_map/all_to_all | solution.py:300
  52.4 2.8 fusion.46
  64.1 4.5 %copy.56 = f32[512,16,128]{2,1,0:T(8,128)} copy(f32[512,16,128]{2,0,1:T(8,128)S(1)} %pad_maximum_fusion) | data formatting | bytes 8388608 | tf_op jit(solution)/shard_map/concatenate.1
  68.7 2.4 concatenate.52.f_ref
  71.1 49.6 %density_outer.1 = (f32[1026,8,128]{2,1,0:T(8,128)S(1)}, f32[17,64,128]{2,1,0:T(8,128)S(1)}) custom-call(s32[1]{0:T(128)} %bitcast.24.count, s32[1024]{0:T(1024)S(1)} %fusion.38.units, f32[1026,8,128]{2,1,0:T(8,128)S(1)} %concatenate.52.f_ref, bf16[48,256]{1,0:T(8,128)(2,1)S(1)} %get-tuple-element.40.pick), custom_call_target="tpu_custom_call" | custom-call | flops 20971520000 | bytes 8404992 | tf_op jit(solution)/shard_map/density_outer/pallas_call | solution.py:222
  133.2 5.5 %all-to-all-start.1 = ((f32[1,256,256]{2,0,1:T(1,128)}), f32[1,256,256]{2,0,1:T(1,128)S(1)}, u32[]{:S(2)}, u32[]{:S(2)}) async-start(f32[1,256,256]{2,0,1:T(1,128)} %copy.58), calls=%async_computation.1 | async-start | bytes 524288 | tf_op jit(solution)/shard_map/all_to_all | solution.py:300
  141.8 20.8 %density_inner.1 = (f32[514,8,128]{2,1,0:T(8,128)S(1)}, f32[9,64,128]{2,1,0:T(8,128)S(1)}) custom-call(s32[1]{0:T(128)} %bitcast.10.count, s32[512]{0:T(512)S(1)} %fusion.39.units, f32[514,8,128]{2,1,0:T(8,128)S(1)} %concatenate.47.f_ref, bf16[48,256]{1,0:T(8,128)(2,1)S(1)} %get-tuple-element.40.pick), custom_call_target="tpu_custom_call" | custom-call | flops 10485760000 | bytes 4210688 | tf_op jit(solution)/shard_map/density_inner/pallas_call | solution.py:222
  162.6 39.2 %density_self.1 = f32[514,8,128]{2,1,0:T(8,128)S(1)} custom-call(s32[1]{0:T(128)} %bitcast.count, s32[1024]{0:T(1024)S(1)} %fusion.37.units, f32[514,8,128]{2,1,0:T(8,128)S(1)} %concatenate.47.f_ref, bf16[48,256]{1,0:T(8,128)(2,1)S(1)} %get-tuple-element.40.pick), custom_call_target="tpu_custom_call" | custom-call | flops 25165824000 | bytes 4210688 | tf_op jit(solution)/shard_map/density_self/pallas_call | solution.py:222
  205.5 2.5 bitcast_dynamic-update-slice_fusion
  213.3 13.0 %all-to-all-start.2 = ((f32[1,256,256]{2,0,1:T(1,128)}), f32[1,256,256]{2,0,1:T(1,128)S(1)}, u32[]{:S(2)}, u32[]{:S(2)}) async-start(f32[1,256,256]{2,0,1:T(1,128)} %copy.61), calls=%async_computation.2 | async-start | bytes 524288 | tf_op jit(solution)/shard_map/all_to_all | solution.py:300
  226.3 57.2 %force_self.1 = f32[514,8,128]{2,1,0:T(8,128)S(1)} custom-call(s32[1]{0:T(128)} %bitcast.count, s32[1024]{0:T(1024)S(1)} %fusion.37.units, f32[514,8,128]{2,1,0:T(8,128)S(1)} %concatenate.55.f_ref, bf16[48,256]{1,0:T(8,128)(2,1)S(1)} %get-tuple-element.39.pick), custom_call_target="tpu_custom_call" | custom-call | flops 25165824000 | bytes 4210688 | tf_op jit(solution)/shard_map/force_self/pallas_call | solution.py:222
  284.8 21.8 %force_inner.1 = f32[514,8,128]{2,1,0:T(8,128)S(1)} custom-call(s32[1]{0:T(128)} %bitcast.10.count, s32[512]{0:T(512)S(1)} %fusion.39.units, f32[514,8,128]{2,1,0:T(8,128)S(1)} %concatenate.55.f_ref, bf16[48,256]{1,0:T(8,128)(2,1)S(1)} %get-tuple-element.39.pick), custom_call_target="tpu_custom_call" | custom-call | flops 10485760000 | bytes 4210688 | tf_op jit(solution)/shard_map/force_inner/pallas_call | solution.py:222
  308.1 2.6 fusion.1
  311.5 2.4 copy.62
  314.3 51.8 %force_outer.1 = f32[1026,8,128]{2,1,0:T(8,128)S(1)} custom-call(s32[1]{0:T(128)} %bitcast.24.count, s32[1024]{0:T(1024)S(1)} %fusion.38.units, f32[1026,8,128]{2,1,0:T(8,128)S(1)} %concatenate.59.f_ref, bf16[48,256]{1,0:T(8,128)(2,1)S(1)} %get-tuple-element.39.pick), custom_call_target="tpu_custom_call" | custom-call | flops 20971520000 | bytes 8404992 | tf_op jit(solution)/shard_map/force_outer/pallas_call | solution.py:222
  366.4 4.2 %copy.63 = f32[8,512,2,128]{3,2,1,0:T(2,128)} copy(f32[8,512,2,128]{3,0,2,1:T(8,128)S(1)} %bitcast.157) | data formatting | bytes 8388608 | tf_op jit(solution)/shard_map/transpose | solution.py:292
  370.6 6.5 %reshape.499 = f32[8,512,256]{2,1,0:T(8,128)} reshape(f32[8,512,2,128]{3,2,1,0:T(2,128)} %copy.63) | data formatting | bytes 8388608 | tf_op jit(solution)/shard_map/reshape | solution.py:292
  380.9 14.7 %all-to-all-start.3 = ((f32[3,256,256]{2,0,1:T(4,128)}), f32[3,256,256]{2,0,1:T(4,128)S(1)}, u32[]{:S(2)}, u32[]{:S(2)}) async-start(f32[3,256,256]{2,0,1:T(4,128)} %copy.64), calls=%async_computation.3 | async-start | bytes 2097152 | tf_op jit(solution)/shard_map/all_to_all | solution.py:300
  397.5 2.4 copy.60
  399.9 2.9 reshape.496
  406.2 8.2 %all-to-all-done.3 = f32[3,256,256]{2,0,1:T(4,128)S(1)} async-done(((f32[3,256,256]{2,0,1:T(4,128)}), f32[3,256,256]{2,0,1:T(4,128)S(1)}, u32[]{:S(2)}, u32[]{:S(2)}) %all-to-all-start.3) | async-done | bytes 786464 | tf_op jit(solution)/shard_map/all_to_all | solution.py:300
  414.4 3.0 fusion.8
  (160 shorter events, 60.9 us)
Async XLA Ops:
  0.6 2.6 copy-start.6
  0.6 3.1 copy-start.21
  10.1 12.3 %copy-start.7 = (f32[3,256,256]{2,1,0:T(8,128)S(1)}, f32[3,256,256]{2,1,0:T(8,128)}, u32[]{:S(2)}) copy-start(f32[3,256,256]{2,1,0:T(8,128)} %param.8) | copy-start | bytes 2359300
  10.1 12.5 %copy-start.22 = (s32[2,384]{1,0:T(2,128)S(1)}, s32[2,384]{1,0:T(2,128)}, u32[]{:S(2)}) copy-start(s32[2,384]{1,0:T(2,128)} %param.13) | copy-start | bytes 9220
  10.1 12.5 %copy-start.20 = (s32[256]{0:T(256)S(1)}, s32[256]{0:T(256)}, u32[]{:S(2)}) copy-start(s32[256]{0:T(256)} %param.12) | copy-start | bytes 3076
  10.1 42.3 %all-to-all-start = ((f32[5,256,256]{2,0,1:T(8,128)}), f32[5,256,256]{2,0,1:T(8,128)}, u32[]{:S(2)}, u32[]{:S(2)}) async-start(f32[5,256,256]{2,0,1:T(8,128)} %select_bitcast_fusion), calls=%async_computation | async-start | bytes 4194304 | tf_op jit(solution)/shard_map/all_to_all | solution.py:300
  61.5 2.3 copy-start.4
  61.5 68.5 %copy-start.3 = (f32[256,8,256]{2,0,1:T(8,128)}, f32[256,8,256]{2,0,1:T(8,128)S(1)}, u32[]{:S(2)}) copy-start(f32[256,8,256]{2,0,1:T(8,128)S(1)} %get-tuple-element.51) | copy-start | bytes 6291460
  132.2 6.5 %copy-start.10 = (f32[512,256]{1,0:T(8,128)}, f32[512,256]{1,0:T(8,128)S(1)}, u32[]{:S(2)}) copy-start(f32[512,256]{1,0:T(8,128)S(1)} %get-tuple-element.17) | copy-start | bytes 1572868
  133.2 71.6 %all-to-all-start.1 = ((f32[1,256,256]{2,0,1:T(1,128)}), f32[1,256,256]{2,0,1:T(1,128)S(1)}, u32[]{:S(2)}, u32[]{:S(2)}) async-start(f32[1,256,256]{2,0,1:T(1,128)} %copy.58), calls=%async_computation.1 | async-start | bytes 524288 | tf_op jit(solution)/shard_map/all_to_all | solution.py:300
  202.6 2.9 copy-start.8
  202.7 2.9 copy-start.11
  203.5 2.0 copy-start.13
  213.3 94.8 %all-to-all-start.2 = ((f32[1,256,256]{2,0,1:T(1,128)}), f32[1,256,256]{2,0,1:T(1,128)S(1)}, u32[]{:S(2)}, u32[]{:S(2)}) async-start(f32[1,256,256]{2,0,1:T(1,128)} %copy.61), calls=%async_computation.2 | async-start | bytes 524288 | tf_op jit(solution)/shard_map/all_to_all | solution.py:300
  283.5 1.3 copy-start
  284.8 23.2 %copy-start.9 = (f32[512,1,256]{2,0,1:T(8,128)S(1)}, f32[512,1,256]{2,0,1:T(8,128)}, u32[]{:S(2)}) copy-start(f32[512,1,256]{2,0,1:T(8,128)} %get-tuple-element.18) | copy-start | bytes 1572868
  306.6 1.4 copy-start.2
  370.6 7.5 %copy-start.16 = (f32[256,1,256]{2,0,1:T(8,128)S(1)}, f32[256,1,256]{2,0,1:T(8,128)}, u32[]{:S(2)}) copy-start(f32[256,1,256]{2,0,1:T(8,128)} %get-tuple-element.31) | copy-start | bytes 786436
  370.6 7.5 %copy-start.17 = (f32[256,1,256]{2,0,1:T(8,128)S(1)}, f32[256,1,256]{2,0,1:T(8,128)}, u32[]{:S(2)}) copy-start(f32[256,1,256]{2,0,1:T(8,128)} %get-tuple-element.32) | copy-start | bytes 786436
  370.6 7.5 %copy-start.18 = (f32[256,1,256]{2,0,1:T(8,128)S(1)}, f32[256,1,256]{2,0,1:T(8,128)}, u32[]{:S(2)}) copy-start(f32[256,1,256]{2,0,1:T(8,128)} %get-tuple-element.33) | copy-start | bytes 786436
  379.4 16.2 %copy-start.1 = (f32[514,8,128]{2,1,0:T(8,128)S(1)}, f32[514,8,128]{2,1,0:T(8,128)}, u32[]{:S(2)}) copy-start(f32[514,8,128]{2,1,0:T(8,128)} %copy-done) | copy-start | bytes 6316036
  380.9 33.5 %all-to-all-start.3 = ((f32[3,256,256]{2,0,1:T(4,128)}), f32[3,256,256]{2,0,1:T(4,128)S(1)}, u32[]{:S(2)}, u32[]{:S(2)}) async-start(f32[3,256,256]{2,0,1:T(4,128)} %copy.64), calls=%async_computation.3 | async-start | bytes 2097152 | tf_op jit(solution)/shard_map/all_to_all | solution.py:300
  402.8 11.6 %copy-start.19 = (f32[256,256]{1,0:T(8,128)S(1)}, f32[256,256]{1,0:T(8,128)}, u32[]{:S(2)}) copy-start(f32[256,256]{1,0:T(8,128)} %fusion.23) | copy-start | bytes 786436
  404.9 1.3 copy-start.5
  (3 other events, 3.1 us)

commit v2 on v1

v2 whole, which is shorter than its diff:
```python
import functools
import math

import jax
import jax.numpy as jnp
from jax import lax
from jax.experimental import pallas as pl
from jax.experimental.pallas import tpu as pltpu
from jax.sharding import PartitionSpec as P

KERNEL_NORM = 21.0 / (2.0 * math.pi)
AXES = ("gx", "gy")
LANES = 128
TILE = 256
ROWS = 64
CHUNKS = TILE // ROWS
TINY = 1e-30
F32 = jnp.float32
BF16 = jnp.bfloat16

ROW_NORM, ROW_ONE, ROW_H, ROW_MASS, ROW_G = 3, 4, 5, 6, 7

NN = (((1,), (0,)), ((), ()))
TN = (((0,), (0,)), ((), ()))
NT = (((1,), (1,)), ((), ()))


def mxu(a, b, dims):
    return lax.dot_general(a, b, dims, preferred_element_type=F32)


def pieces3(x):
    a = x.astype(BF16).astype(F32)
    r = x - a
    b = r.astype(BF16).astype(F32)
    c = r - b
    return a, b, c


def left_stack(x):
    a, b, c = pieces3(x)
    return jnp.concatenate([a, a, b, b, a, c], axis=0).astype(BF16)


def right_stack(x):
    a, b, c = pieces3(x)
    return jnp.concatenate([a, b, a, b, c, a], axis=0).astype(BF16)


def hi_lo_rows(x):
    hi = x.astype(BF16).astype(F32)
    return jnp.concatenate([hi, x - hi], axis=0).astype(BF16)


def twice(x):
    return jnp.concatenate([x, x], axis=1)


def row_fields(f_ref, i):
    block = f_ref[i >> 2, (i >> 1) & 1]
    return pltpu.roll(block, (i & 1) * ROWS, axis=1)[:, :ROWS]


def lane_fields(f_ref, j):
    return jnp.concatenate([f_ref[j, 0], f_ref[j, 1]], axis=1)


def distances(f_ref, pick, i, j):
    left = left_stack(row_fields(f_ref, i))
    lanes = lane_fields(f_ref, j)
    row = lax.broadcasted_iota(jnp.int32, (8, TILE), 0)
    norm = lanes[ROW_NORM : ROW_NORM + 1, :]
    right = jnp.where(row < 3, -2.0 * lanes, jnp.where(row == ROW_ONE, norm, jnp.where(row == ROW_NORM, 1.0, 0.0)))
    return mxu(left, right_stack(right), TN), mxu(left, pick, TN)


def lane_row(f_ref, j, which):
    return jnp.concatenate([f_ref[j, 0, which : which + 1, :], f_ref[j, 1, which : which + 1, :]], axis=1)


def fold_rows(x):
    total = x[0:8]
    for k in range(1, x.shape[0] // 8):
        total = total + x[8 * k : 8 * k + 8]
    return total


def add_lanes(out, j, values):
    out[j, 0] += values[:, :LANES]
    out[j, 1] += values[:, LANES:]


def add_rows(out, i, values):
    lane = lax.broadcasted_iota(jnp.int32, (8, LANES), 1)
    out[i >> 2, (i >> 1) & 1] += jnp.where((lane >> 6) == (i & 1), twice(values), 0.0)


def root(squared):
    squared = jnp.maximum(squared, TINY)
    return squared * lax.rsqrt(squared)


def density_self_values(parts, f_ref, i, j):
    squared, column = parts
    dist = root(squared)
    h = lane_row(f_ref, j, ROW_H)
    t = jnp.maximum(h - dist, 0.0)
    t = t * t
    return fold_rows(t * t * (h + 4.0 * dist) * twice(column))


def density_pair_values(parts, f_ref, i, j):
    squared, column = parts
    dist = root(squared)
    four = 4.0 * dist
    h_row, m_row = twice(column[:, :LANES]), twice(column[:, LANES:])
    h, m = lane_row(f_ref, j, ROW_H), lane_row(f_ref, j, ROW_MASS)
    t = jnp.maximum(h_row - dist, 0.0)
    t = t * t
    near = t * t * (h_row + four) * m
    s = jnp.maximum(h - dist, 0.0)
    s = s * s
    far = s * s * (h + four) * m_row
    return hi_lo(near[:, :LANES] + near[:, LANES:]), fold_rows(far)


def density_pair_store(values, out, i, j):
    (hi, lo), far = values
    add_lanes(out, j, far)
    one = (lax.broadcasted_iota(jnp.int32, (16, LANES), 0) == 0).astype(BF16)
    add_rows(out, i, (mxu(one, hi, NT) + mxu(one, lo, NT))[0:8])


def hi_lo(x):
    hi = x.astype(BF16)
    return hi, (x - hi.astype(F32)).astype(BF16)


def force_values(parts, f_ref, i, j):
    squared, column = parts
    dist = root(squared)
    h_row, g_row = twice(column[:, :LANES]), twice(column[:, LANES:])
    h, g = lane_row(f_ref, j, ROW_H), lane_row(f_ref, j, ROW_G)
    a = jnp.maximum(h_row - dist, 0.0)
    b = jnp.maximum(h - dist, 0.0)
    return hi_lo(g_row * (a * a * a) + g * (b * b * b))


def moments(x):
    return hi_lo_rows(x * x[ROW_MASS : ROW_MASS + 1, :])


def force_store(both, values, f_ref, out, i, j):
    hi, lo = values
    rows = moments(row_fields(f_ref, i))
    add_lanes(out, j, fold_rows(mxu(rows, hi, NN) + mxu(rows, lo, NN)))
    if both:
        lanes = moments(lane_fields(f_ref, j))
        add_rows(out, i, fold_rows(mxu(lanes, hi, NT) + mxu(lanes, lo, NT)))


def sweep(unroll, lead, lag, count, units, stage_a, stage_b, stage_c):
    def body(step, carry):
        ids = []
        for k in range(unroll):
            code = units[step * unroll + k]
            ids.append((code >> 16, code & 0xFFFF))
        parts, values = {}, {}
        for k in range(-lead, unroll + lag):
            if 0 <= k + lead < unroll:
                parts[k + lead] = stage_a(*ids[k + lead])
            if 0 <= k < unroll:
                values[k] = stage_b(parts.pop(k), *ids[k])
            if 0 <= k - lag < unroll:
                stage_c(values.pop(k - lag), *ids[k - lag])
        return carry

    lax.fori_loop(0, count, body, 0)


def sweep_density(unroll, both, count, units, f_ref, pick, out):
    out[...] = jnp.zeros_like(out)
    if both:
        sweep(
            unroll, 2, 2, count[0], units,
            lambda i, j: distances(f_ref, pick[...], i, j),
            lambda p, i, j: density_pair_values(p, f_ref, i, j),
            lambda v, i, j: density_pair_store(v, out, i, j),
        )
    else:
        sweep(
            unroll, 2, 1, count[0], units,
            lambda i, j: distances(f_ref, pick[:, LANES:], i, j),
            lambda p, i, j: density_self_values(p, f_ref, i, j),
            lambda v, i, j: add_lanes(out, j, v),
        )


def sweep_force(unroll, both, count, units, f_ref, pick, out):
    out[...] = jnp.zeros_like(out)
    sweep(
        unroll, 2, 2, count[0], units,
        lambda i, j: distances(f_ref, pick[...], i, j),
        lambda p, i, j: force_values(p, f_ref, i, j),
        lambda v, i, j: force_store(both, v, f_ref, out, i, j),
    )


def density_scale(h):
    h2 = h * h
    h4 = h2 * h2
    return KERNEL_NORM / (h4 * h4)


def each_group(cells, body):
    def step(k, carry):
        for half in range(2):
            body(pl.multiple_of(k * 8, 8), half)
        return carry

    lax.fori_loop(0, cells // 8, step, 0)


def half_lanes(half):
    return slice(half * LANES, (half + 1) * LANES)


def prepare_kernel(counts, targets, pos, smooth, masses, fields, outgoing):
    cells = smooth.shape[0]
    fields[cells] = jnp.zeros((2, 8, LANES), F32)
    sub = lax.broadcasted_iota(jnp.int32, (8, LANES), 0)
    lane = lax.broadcasted_iota(jnp.int32, (8, LANES), 1)

    def group(c, half):
        count = jnp.zeros((8, LANES), jnp.int32)
        for k in range(8):
            count = jnp.where(sub == k, counts[c + k], count)
        at = (pl.ds(c, 8), half_lanes(half))
        x, y, z = (pos[k, at[0], at[1]] - 0.5 for k in range(3))
        mass = jnp.where(lane + half * LANES < count, masses[at], 0.0)
        rows = (x, y, z, x * x + y * y + z * z, jnp.ones_like(x), smooth[at], mass, count.astype(F32))
        for k in range(8):
            fields[pl.ds(c, 8), half, k, :] = rows[k]

    each_group(cells, group)

    def export(k, carry):
        for s in range(8):
            slot = k * 8 + s
            outgoing[slot] = fields[jnp.maximum(targets[slot], 0)]
        return carry

    lax.fori_loop(0, outgoing.shape[0] // 8, export, 0)


def density_inner_kernel(unroll, both, count, units, f_ref, pick, out):
    sweep_density(unroll, both, count, units, f_ref, pick, out)


def load_all(own, ghosts, everything, sems):
    first = own.shape[0]
    copies = [
        pltpu.make_async_copy(own, everything.at[pl.ds(0, first)], sems.at[0]),
        pltpu.make_async_copy(ghosts, everything.at[pl.ds(first, ghosts.shape[0])], sems.at[1]),
    ]
    for copy in copies:
        copy.start()
    for copy in copies:
        copy.wait()


def density_outer_kernel(unroll, count, units, own, ghosts, pick, own_out, ghost_out, everything, acc, sems):
    load_all(own, ghosts, everything, sems)
    sweep_density(unroll, True, count, units, everything, pick, acc)
    first = own.shape[0]

    def finish_own(c, half):
        own_out[pl.ds(c, 8), half_lanes(half)] = jnp.sum(acc[pl.ds(c, 8), half], axis=1)

    def finish_ghost(c, half):
        total = jnp.sum(acc[pl.ds(first + c, 8), half], axis=1)
        scale = density_scale(everything[pl.ds(first + c, 8), half, ROW_H, :])
        ghost_out[pl.ds(c, 8), 0, half_lanes(half)] = total * scale

    each_group(own_out.shape[0], finish_own)
    each_group(ghost_out.shape[0], finish_ghost)


def factor_kernel(targets, self_acc, inner_acc, outer, returned, fields, entropy, density, fields_g, outgoing, total, scaled, g_all):
    cells = density.shape[0]
    fields_g[...] = fields[...]

    def gather(c, half):
        at = (pl.ds(c, 8), half_lanes(half))
        both = jnp.sum(self_acc[pl.ds(c, 8), half] + inner_acc[pl.ds(c, 8), half], axis=1) + outer[at]
        scale = density_scale(fields[pl.ds(c, 8), half, ROW_H, :])
        total[at] = both * scale
        scaled[at] = 20.0 * scale

    each_group(cells, gather)

    def credit(k, carry):
        for s in range(8):
            slot = k * 8 + s
            target = targets[slot]
            at = pl.ds(jnp.where(target < 0, cells, target), 1)
            total[at, :] += returned[slot]
        return carry

    lax.fori_loop(0, returned.shape[0] // 8, credit, 0)

    def finish(c, half):
        at = (pl.ds(c, 8), half_lanes(half))
        live = fields[pl.ds(c, 8), half, ROW_MASS, :] > 0.0
        rho = jnp.where(live, total[at], 0.0)
        density[at] = rho
        safe = jnp.where(live, rho, 1.0)
        g = jnp.where(live, entropy[at] * jnp.exp(jnp.log(safe) * (-1.0 / 3.0)) * scaled[at], 0.0)
        g_all[at] = g
        fields_g[pl.ds(c, 8), half, ROW_G, :] = g

    each_group(cells, finish)

    def export(k, carry):
        for s in range(8):
            slot = k * 8 + s
            outgoing[slot] = g_all[pl.ds(jnp.maximum(targets[slot], 0), 1), :]
        return carry

    lax.fori_loop(0, outgoing.shape[0] // 8, export, 0)


def accelerate(f_ref, sums, c, half):
    f, s = f_ref[c, half], sums[c, half]
    return f * s[ROW_ONE : ROW_ONE + 1, :] - s


def force_inner_kernel(unroll, both, count, units, f_ref, pick, out):
    sweep_force(unroll, both, count, units, f_ref, pick, out)

    def finish(k, carry):
        for s in range(4):
            for half in range(2):
                out[4 * k + s, half] = accelerate(f_ref, out, 4 * k + s, half)
        return carry

    lax.fori_loop(0, out.shape[0] // 4, finish, 0)


def force_outer_kernel(unroll, count, units, own, ghosts, ghost_g, pick, own_out, ghost_out, everything, acc, sems):
    load_all(own, ghosts, everything, sems)
    first = own.shape[0]

    def insert(c, half):
        everything[pl.ds(first + c, 8), half, ROW_G, :] = ghost_g[pl.ds(c, 8), 0, half_lanes(half)]

    each_group(ghost_g.shape[0], insert)
    sweep_force(unroll, True, count, units, everything, pick, acc)

    def finish(k, carry):
        for s in range(4):
            for half in range(2):
                own_out[4 * k + s, half] = accelerate(everything, acc, 4 * k + s, half)
                ghost_out[4 * k + s, half] = accelerate(everything, acc, first + 4 * k + s, half)[0:4]
        return carry

    lax.fori_loop(0, own_out.shape[0] // 4, finish, 0)


def final_kernel(targets, self_acc, inner_acc, outer_acc, returned, fields, acceleration, total):
    cells = outer_acc.shape[0]

    def gather(k, carry):
        for s in range(4):
            c = 4 * k + s
            total[c] = self_acc[c] + inner_acc[c] + outer_acc[c]
        return carry

    lax.fori_loop(0, cells // 4, gather, 0)

    def credit(k, carry):
        for s in range(8):
            slot = k * 8 + s
            target = targets[slot]
            at = jnp.where(target < 0, cells, target)
            for half in range(2):
                total[at, half, 0:4, :] += returned[slot, half]
        return carry

    lax.fori_loop(0, returned.shape[0] // 8, credit, 0)

    def finish(c, half):
        live = fields[pl.ds(c, 8), half, ROW_MASS, :] > 0.0
        for k in range(3):
            acceleration[k, pl.ds(c, 8), half_lanes(half)] = jnp.where(live, total[pl.ds(c, 8), half, k, :], 0.0)

    each_group(cells, finish)


SMEM = pl.BlockSpec(memory_space=pltpu.SMEM)
VMEM = pl.BlockSpec(memory_space=pltpu.VMEM)
ANY = pl.BlockSpec(memory_space=pl.ANY)


def launch(body, name, in_specs, shapes, args, scratch=(), flops=0, limit=40):
    return pl.pallas_call(
        body,
        out_shape=[jax.ShapeDtypeStruct(shape, F32) for shape in shapes],
        in_specs=in_specs,
        out_specs=[VMEM] * len(shapes),
        scratch_shapes=list(scratch),
        name=name,
        compiler_params=pltpu.CompilerParams(vmem_limit_bytes=limit * 1024 * 1024),
        cost_estimate=pl.CostEstimate(flops=flops, bytes_accessed=1 << 21, transcendentals=0),
    )(*args)


def pick_matrix(second):
    k = lax.broadcasted_iota(jnp.int32, (48, TILE), 0)
    lane = lax.broadcasted_iota(jnp.int32, (48, TILE), 1)
    group, row = k // 8, k % 8
    used = (group == 0) | (group == 2) | (group == 5)
    return (used & (row == jnp.where(lane < LANES, ROW_H, second))).astype(BF16)


def compact(valid, code, spare, unroll):
    num = valid.shape[0]
    flags = valid.astype(jnp.int32)
    ids = jnp.arange(num, dtype=jnp.int32)
    rank = jnp.sum(jnp.where(ids[None, :] < ids[:, None], flags[None, :], 0), axis=1)
    total = jnp.sum(flags)
    hit = (rank[None, :] == ids[:, None]) & valid[None, :]
    listed = jnp.sum(jnp.where(hit, code[None, :], 0), axis=1)
    listed = jnp.where(ids < total, listed, spare)
    return listed.astype(jnp.int32), ((total + unroll - 1) // unroll).reshape(1).astype(jnp.int32)


def look_up(table, ids):
    slots = jnp.arange(table.shape[0], dtype=jnp.int32)
    return jnp.sum(jnp.where(ids[:, None] == slots[None, :], table[None, :], 0), axis=1)


def pair_units(first, second, live, counts, spare, unroll):
    n_first, n_second = look_up(counts, first), look_up(counts, second)
    swap = n_second < n_first
    rows = jnp.where(swap, second, first)
    lanes = jnp.where(swap, first, second)
    chunks = (jnp.minimum(n_first, n_second) + ROWS - 1) // ROWS
    step = jnp.arange(CHUNKS, dtype=jnp.int32)
    valid = (step[None, :] < chunks[:, None]) & live[:, None]
    code = ((rows[:, None] * CHUNKS + step[None, :]) << 16) | lanes[:, None]
    return compact(valid.reshape(-1), code.reshape(-1), spare, unroll)


def trade(payload):
    return lax.all_to_all(payload, AXES, split_axis=0, concat_axis=0, tiled=True)


def local(positions, smooth, masses, entropy, cell_counts, cell_pairs, pair_count, send_cells):
    cells, tile = smooth.shape
    num_pairs = cell_pairs.shape[1]
    slots = send_cells.shape[1]
    unroll = 32
    targets = send_cells[0]
    padded = (cells + 1, 2, 8, LANES)
    whole = (cells + 1 + slots, 2, 8, LANES)
    pick_m, pick_g = pick_matrix(ROW_MASS), pick_matrix(ROW_G)
    spare = ((cells * CHUNKS) << 16) | cells
    unit = ROWS * TILE * 2000
    both_sems = pltpu.SemaphoreType.DMA((2,))

    own, outgoing = launch(
        prepare_kernel, "prepare", [SMEM, SMEM, VMEM, VMEM, VMEM], [padded, (slots, 2, 8, LANES)],
        (cell_counts, targets, positions, smooth, masses),
    )
    ghosts = trade(outgoing)

    step = jnp.arange(CHUNKS, dtype=jnp.int32)
    ids = jnp.arange(cells, dtype=jnp.int32)
    self_valid = step[None, :] < ((cell_counts + ROWS - 1) // ROWS)[:, None]
    self_code = ((ids[:, None] * CHUNKS + step[None, :]) << 16) | ids[:, None]
    self_units, self_count = compact(self_valid.reshape(-1), self_code.reshape(-1), spare, unroll)
    live_pair = jnp.arange(num_pairs, dtype=jnp.int32) < pair_count[0]
    first, second = cell_pairs[0], cell_pairs[1]
    second = jnp.where(second < cells, second, second + 1)
    inner_units, inner_count = pair_units(first[slots:], second[slots:], live_pair[slots:], cell_counts, spare, unroll)

    (self_rho,) = launch(
        functools.partial(density_inner_kernel, unroll, False), "density_self", [SMEM, SMEM, VMEM, VMEM], [padded],
        (self_count, self_units, own, pick_m), flops=768 * unit,
    )
    ghosts, self_rho = lax.optimization_barrier((ghosts, self_rho))

    ghost_counts = ghosts[:, 0, ROW_G, 0].astype(jnp.int32)
    all_counts = jnp.concatenate([cell_counts, jnp.zeros((1,), jnp.int32), ghost_counts])
    outer_units, outer_count = pair_units(first[:slots], second[:slots], live_pair[:slots], all_counts, spare, unroll)
    outer_rho, ghost_rho = launch(
        functools.partial(density_outer_kernel, unroll), "density_outer", [SMEM, SMEM, ANY, ANY, VMEM],
        [(cells, tile), (slots, 1, tile)], (outer_count, outer_units, own, ghosts, pick_m),
        scratch=[pltpu.VMEM(whole, F32), pltpu.VMEM(whole, F32), both_sems], flops=640 * unit,
    )
    returned_rho = trade(ghost_rho)
    (inner_rho,) = launch(
        functools.partial(density_inner_kernel, unroll, True), "density_inner", [SMEM, SMEM, VMEM, VMEM], [padded],
        (inner_count, inner_units, own, pick_m), flops=320 * unit,
    )
    returned_rho, inner_rho = lax.optimization_barrier((returned_rho, inner_rho))

    density, own_g, outgoing_g = launch(
        factor_kernel, "factor", [SMEM] + [VMEM] * 6, [(cells, tile), padded, (slots, 1, tile)],
        (targets, self_rho, inner_rho, outer_rho, returned_rho, own, entropy),
        scratch=[pltpu.VMEM((cells + 8, tile), F32)] * 3,
    )
    ghost_g = trade(outgoing_g)
    (self_acc,) = launch(
        functools.partial(force_inner_kernel, unroll, False), "force_self", [SMEM, SMEM, VMEM, VMEM], [padded],
        (self_count, self_units, own_g, pick_g), flops=768 * unit,
    )
    ghost_g, self_acc = lax.optimization_barrier((ghost_g, self_acc))

    outer_acc, ghost_acc = launch(
        functools.partial(force_outer_kernel, unroll), "force_outer", [SMEM, SMEM, ANY, ANY, VMEM, VMEM],
        [(cells, 2, 8, LANES), (slots, 2, 4, LANES)], (outer_count, outer_units, own_g, ghosts, ghost_g, pick_g),
        scratch=[pltpu.VMEM(whole, F32), pltpu.VMEM(whole, F32), both_sems], flops=640 * unit,
    )
    returned_acc = trade(ghost_acc)
    (inner_acc,) = launch(
        functools.partial(force_inner_kernel, unroll, True), "force_inner", [SMEM, SMEM, VMEM, VMEM], [padded],
        (inner_count, inner_units, own_g, pick_g), flops=320 * unit,
    )
    returned_acc, inner_acc = lax.optimization_barrier((returned_acc, inner_acc))

    (acceleration,) = launch(
        final_kernel, "final", [SMEM] + [VMEM] * 5, [(3, cells, tile)],
        (targets, self_acc, inner_acc, outer_acc, returned_acc, own), scratch=[pltpu.VMEM(padded, F32)],
    )
    return (density, acceleration)


def solution(mesh):
    in_specs = (
        P(None, AXES, None),
        P(AXES, None),
        P(AXES, None),
        P(AXES, None),
        P(AXES),
        P(None, AXES),
        P(AXES),
        P(AXES, None),
    )
    out_specs = (P(AXES, None), P(None, AXES, None))
    return jax.shard_map(local, mesh=mesh, in_specs=in_specs, out_specs=out_specs, check_vma=False)
```

time: 422 us -> 332 us (0.79)
  local copies, waits for them, and re-layouts: 64.6 us -> 28.1 us
  waiting for transfers between devices: 27.1 us -> 0.01 us
  other arithmetic: 30.3 us -> 14 us
  matrix products: 5.48 us -> 0 us
    all_to_all x4, waiting for transfers between devices: 27.1 us -> 0.01 us  [trade(): lax.all_to_all(payload, AXES, split_axis=0, concat_axis=0, tiled=True)]
    unnamed x59 -> x50, local copies, waits for them, and re-layouts: 6.94 us -> 27.3 us
    slice x10 -> x3, local copies, waits for them, and re-layouts: 12.5 us -> 0.03 us  [the longest x1 0.02 us: local(): first, second = (cell_pairs[0], cell_pairs[1])]
    another operation x8 -> x0, local copies, waits for them, and re-layouts: 12.1 us -> none
    reshape x2 -> x0, local copies, waits for them, and re-layouts: 9.44 us -> none  [from_blocks(): blocks[:2 * cells].reshape(cells, 2, 8, LANES).transpose(2, 0, 1, 3)]
    transpose x2 -> x0, local copies, waits for them, and re-layouts: 6.62 us -> none  [from_blocks(): blocks[:2 * cells].reshape(cells, 2, 8, LANES).transpose(2, 0, 1, 3)]
    dot_general x2 -> x0, matrix products: 5.48 us -> none  [the longest x1 3.02 us: local(): jnp.einsum('cg,kgp->kcp', selector, returned_acc, precision=lax.Precision...]
    concatenate x5 -> x1, other arithmetic: 5.38 us -> 0.08 us  [local(): jnp.concatenate([cell_counts, jnp.zeros((1,), jnp.int32), ghost_counts])]
  transfers between devices with their start and end apart: 4 -> 4, of which waited for: 2 -> 0; matrix products, arithmetic and copies ran while one was open for 6% -> 2% of each run, Pallas kernels for 33% -> 37%
where the time goes in v2:
time: 332 us; the launch traced here: 328 us
  Pallas kernels  236 us (71%)
  starting transfers between devices  46.3 us (14%)
  local copies, waits for them, and re-layouts  28.1 us (8%)
  other arithmetic  14 us (4%)
  between operations  3.75 us (1%)
    pallas_call x9, Pallas kernels, launch(): pl.pallas_call(body, out_shape=[jax.ShapeDtypeStruct(shape, F32) for shap...  236 us
    all_to_all x4, starting transfers between devices, trade(): lax.all_to_all(payload, AXES, split_axis=0, concat_axis=0, tiled=True)  46.3 us
    unnamed x50, local copies, waits for them, and re-layouts  27.3 us
  transfers between devices with their start and end apart: 4, of which 0 were waited for; matrix products, arithmetic and copies ran while one was open for 2% of the time, Pallas kernels for 37%

profile of v2, /device:TPU:1, one launch (start us, length us, event | category | flops | bytes accessed | tf_op | source)
XLA Modules:
  0.0 328.1 jit_solution(13986565077428215566)
XLA Ops:
  5.0 2.5 prepare.1
  8.9 12.0 %all-to-all-start = ((f32[256,2,8,128]{3,2,1,0:T(8,128)}), f32[256,2,8,128]{3,2,1,0:T(8,128)}, u32[]{:S(2)}, u32[]{:S(2)}) async-start(f32[256,2,8,128]{3,2,1,0:T(8,128)} %copy-done.8), calls=%async_computation | async-start | bytes 4194304 | tf_op jit(solution)/shard_map/all_to_all | solution.py:456
  28.5 33.6 %density_self.1.self_acc = f32[257,2,8,128]{3,2,1,0:T(8,128)S(1)} custom-call(s32[1]{0:T(128)} %bitcast.1.count, s32[1024]{0:T(1024)S(1)} %fusion.11.units, f32[257,2,8,128]{3,2,1,0:T(8,128)S(1)} %get-tuple-element.20.f_ref.own.fields, bf16[48,256]{1,0:T(8,128)(2,1)S(1)} %get-tuple-element.45.pick), custom_call_target="tpu_custom_call" | custom-call | flops 25165824000 | bytes 2097152 | tf_op jit(solution)/shard_map/density_self/pallas_call | solution.py:406
  62.1 1.3 copy-done.4
  63.5 5.8 %convert_reduce_fusion.1 = s32[256]{0:T(256)S(1)} fusion(f32[256,2,8,128]{3,2,1,0:T(8,128)} %all-to-all-done.ghosts), kind=kLoop, calls=%fused_computation.24 | loop fusion | flops 256 | bytes 2048 | tf_op jit(solution)/shard_map/convert_element_type | solution.py:494
  73.5 52.3 %density_outer.1 = (f32[256,256]{1,0:T(8,128)S(1)}, f32[256,1,256]{2,1,0:T(1,128)}) custom-call(s32[1]{0:T(128)} %bitcast.4.count, s32[1024]{0:T(1024)S(1)} %fusion.12.units, f32[257,2,8,128]{3,2,1,0:T(8,128)S(1)} %get-tuple-element.20.f_ref.own.fields, f32[256,2,8,128]{3,2,1,0:T(8,128)} %all-to-all-done.ghosts, bf16[48,256]{1,0:T(8,128)(2,1)S(1)} %get-tuple-element.45.pick), custom_call_target="tpu_custom_call" | custom-call | flops 20971520000 | bytes 2097152 | tf_op jit(solution)/shard_map/density_outer/pallas_call | solution.py:406
  125.8 11.5 %all-to-all-start.1 = ((f32[256,1,256]{2,1,0:T(1,128)}), f32[256,1,256]{2,1,0:T(1,128)S(1)}, u32[]{:S(2)}, u32[]{:S(2)}) async-start(f32[256,1,256]{2,1,0:T(1,128)} %get-tuple-element.23), calls=%async_computation.1 | async-start | bytes 524288 | tf_op jit(solution)/shard_map/all_to_all | solution.py:456
  137.3 20.8 %density_inner.1.inner_acc = f32[257,2,8,128]{3,2,1,0:T(8,128)S(1)} custom-call(s32[1]{0:T(128)} %bitcast.6.count, s32[512]{0:T(512)S(1)} %fusion.13.units, f32[257,2,8,128]{3,2,1,0:T(8,128)S(1)} %get-tuple-element.20.f_ref.own.fields, bf16[48,256]{1,0:T(8,128)(2,1)S(1)} %get-tuple-element.45.pick), custom_call_target="tpu_custom_call" | custom-call | flops 10485760000 | bytes 2097152 | tf_op jit(solution)/shard_map/density_inner/pallas_call | solution.py:406
  159.4 1.6 copy-done.5
  161.0 1.6 copy-done.7
  162.6 6.1 %factor.1 = (f32[256,256]{1,0:T(8,128)}, f32[257,2,8,128]{3,2,1,0:T(8,128)S(1)}, f32[256,1,256]{2,1,0:T(1,128)}) custom-call(s32[256]{0:T(256)S(1)} %bitcast.15, f32[257,2,8,128]{3,2,1,0:T(8,128)S(1)} %copy-done.5, f32[257,2,8,128]{3,2,1,0:T(8,128)S(1)} %copy-done.7, f32[256,256]{1,0:T(8,128)S(1)} %get-tuple-element.25.outer, ...), custom_call_target="tpu_custom_call" | custom-call | bytes 2097152 | tf_op jit(solution)/shard_map/factor/pallas_call | solution.py:406
  170.0 11.5 %all-to-all-start.2 = ((f32[256,1,256]{2,1,0:T(1,128)}), f32[256,1,256]{2,1,0:T(1,128)S(1)}, u32[]{:S(2)}, u32[]{:S(2)}) async-start(f32[256,1,256]{2,1,0:T(1,128)} %get-tuple-element.28), calls=%async_computation.2 | async-start | bytes 524288 | tf_op jit(solution)/shard_map/all_to_all | solution.py:456
  181.5 1.6 copy-done.21
  183.1 48.2 %force_self.1.self_acc = f32[257,2,8,128]{3,2,1,0:T(8,128)S(1)} custom-call(s32[1]{0:T(128)} %bitcast.1.count, s32[1024]{0:T(1024)S(1)} %fusion.11.units, f32[257,2,8,128]{3,2,1,0:T(8,128)S(1)} %copy-done.21, bf16[48,256]{1,0:T(8,128)(2,1)S(1)} %get-tuple-element.44.pick), custom_call_target="tpu_custom_call" | custom-call | flops 25165824000 | bytes 2097152 | tf_op jit(solution)/shard_map/force_self/pallas_call | solution.py:406
  231.3 1.3 copy-done
  232.6 1.6 copy-done.22
  234.2 48.4 %force_outer.1 = (f32[256,2,8,128]{3,2,1,0:T(8,128)S(1)}, f32[256,2,4,128]{3,2,1,0:T(4,128)S(1)}) custom-call(s32[1]{0:T(128)} %bitcast.4.count, s32[1024]{0:T(1024)S(1)} %fusion.12.units, f32[257,2,8,128]{3,2,1,0:T(8,128)S(1)} %copy-done.22, f32[256,2,8,128]{3,2,1,0:T(8,128)} %all-to-all-done.ghosts, f32[256,1,256]{2,1,0:T(1,128)S(1)} %all-to-all-done.2.ghost_g, ...), custom_call_target="tpu_custom_call" | custom-call | flops 20971520000 | bytes 2097152 | tf_op jit(solution)/shard_map/force_outer/pallas_call | solution.py:406
  284.9 11.3 %all-to-all-start.3 = ((f32[256,2,4,128]{3,2,1,0:T(4,128)}), f32[256,2,4,128]{3,2,1,0:T(4,128)S(1)}, u32[]{:S(2)}, u32[]{:S(2)}) async-start(f32[256,2,4,128]{3,2,1,0:T(4,128)} %copy-done.11), calls=%async_computation.3 | async-start | bytes 2097152 | tf_op jit(solution)/shard_map/all_to_all | solution.py:456
  296.2 1.6 copy-done.23
  297.8 20.4 %force_inner.1.inner_acc = f32[257,2,8,128]{3,2,1,0:T(8,128)S(1)} custom-call(s32[1]{0:T(128)} %bitcast.6.count, s32[512]{0:T(512)S(1)} %fusion.13.units, f32[257,2,8,128]{3,2,1,0:T(8,128)S(1)} %copy-done.23, bf16[48,256]{1,0:T(8,128)(2,1)S(1)} %get-tuple-element.44.pick), custom_call_target="tpu_custom_call" | custom-call | flops 10485760000 | bytes 2097152 | tf_op jit(solution)/shard_map/force_inner/pallas_call | solution.py:406
  319.6 1.6 copy-done.1
  321.1 1.6 copy-done.3
  322.7 1.6 copy-done.10
  324.3 3.8 %final.1 = f32[3,256,256]{2,1,0:T(8,128)} custom-call(s32[256]{0:T(256)S(1)} %bitcast.16, f32[257,2,8,128]{3,2,1,0:T(8,128)S(1)} %copy-done.1, f32[257,2,8,128]{3,2,1,0:T(8,128)S(1)} %copy-done.3, f32[256,2,8,128]{3,2,1,0:T(8,128)S(1)} %copy-done.10, f32[256,2,4,128]{3,2,1,0:T(4,128)S(1)} %all-to-all-done.3.returned, ...), custom_call_target="tpu_custom_call" | custom-call | bytes 2097152 | tf_op jit(solution)/shard_map/final/pallas_call | solution.py:406
  (91 shorter events, 20.9 us)
Async XLA Ops:
  0.6 1.1 copy-start.12
  7.5 1.3 copy-start.8
  8.9 12.0 %copy-start.17 = (s32[256]{0:T(256)S(1)}, s32[256]{0:T(256)}, u32[]{:S(2)}) copy-start(s32[256]{0:T(256)} %counts.1) | copy-start | bytes 3076
  8.9 13.4 %copy-start.24 = (s32[2,384]{1,0:T(2,128)S(1)}, s32[2,384]{1,0:T(2,128)}, u32[]{:S(2)}) copy-start(s32[2,384]{1,0:T(2,128)} %param.13) | copy-start | bytes 9220
  8.9 54.6 %all-to-all-start = ((f32[256,2,8,128]{3,2,1,0:T(8,128)}), f32[256,2,8,128]{3,2,1,0:T(8,128)}, u32[]{:S(2)}, u32[]{:S(2)}) async-start(f32[256,2,8,128]{3,2,1,0:T(8,128)} %copy-done.8), calls=%async_computation | async-start | bytes 4194304 | tf_op jit(solution)/shard_map/all_to_all | solution.py:456
  62.1 1.3 copy-start.4
  125.8 33.6 %all-to-all-start.1 = ((f32[256,1,256]{2,1,0:T(1,128)}), f32[256,1,256]{2,1,0:T(1,128)S(1)}, u32[]{:S(2)}, u32[]{:S(2)}) async-start(f32[256,1,256]{2,1,0:T(1,128)} %get-tuple-element.23), calls=%async_computation.1 | async-start | bytes 524288 | tf_op jit(solution)/shard_map/all_to_all | solution.py:456
  137.3 22.2 %copy-start.15 = (f32[256,256]{1,0:T(8,128)S(1)}, f32[256,256]{1,0:T(8,128)}, u32[]{:S(2)}) copy-start(f32[256,256]{1,0:T(8,128)} %entropy.1) | copy-start | bytes 786436
  137.3 22.1 %copy-start.19 = (s32[1,256]{1,0:T(1,128)S(1)}, s32[1,256]{1,0:T(1,128)}, u32[]{:S(2)}) copy-start(s32[1,256]{1,0:T(1,128)} %param.15) | copy-start | bytes 3076
  158.1 1.3 copy-start.6
  159.4 1.6 copy-start.5
  161.0 1.6 copy-start.7
  168.7 1.3 copy-start.20
  170.0 62.7 %all-to-all-start.2 = ((f32[256,1,256]{2,1,0:T(1,128)}), f32[256,1,256]{2,1,0:T(1,128)S(1)}, u32[]{:S(2)}, u32[]{:S(2)}) async-start(f32[256,1,256]{2,1,0:T(1,128)} %get-tuple-element.28), calls=%async_computation.2 | async-start | bytes 524288 | tf_op jit(solution)/shard_map/all_to_all | solution.py:456
  181.5 1.6 copy-start.21
  231.3 1.3 copy-start
  232.6 1.6 copy-start.22
  282.6 1.3 copy-start.9
  284.9 34.6 %all-to-all-start.3 = ((f32[256,2,4,128]{3,2,1,0:T(4,128)}), f32[256,2,4,128]{3,2,1,0:T(4,128)S(1)}, u32[]{:S(2)}, u32[]{:S(2)}) async-start(f32[256,2,4,128]{3,2,1,0:T(4,128)} %copy-done.11), calls=%async_computation.3 | async-start | bytes 2097152 | tf_op jit(solution)/shard_map/all_to_all | solution.py:456
  296.2 1.6 copy-start.23
  318.2 1.3 copy-start.2
  319.5 1.6 copy-start.1
  321.1 1.6 copy-start.3
  322.7 1.6 copy-start.10
  (5 other events, 4.3 us)

commit v3 on v2

v3 whole, which is shorter than its diff:
```python
import functools
import math

import jax
import jax.numpy as jnp
from jax import lax
from jax.experimental import pallas as pl
from jax.experimental.pallas import tpu as pltpu
from jax.sharding import PartitionSpec as P

KERNEL_NORM = 21.0 / (2.0 * math.pi)
AXES = ("gx", "gy")
LANES = 128
TILE = 256
ROWS = 64
CHUNKS = TILE // ROWS
TINY = 1e-30
F32 = jnp.float32
BF16 = jnp.bfloat16

ROW_NORM, ROW_ONE, ROW_H, ROW_MASS, ROW_G = 3, 4, 5, 6, 7

NN = (((1,), (0,)), ((), ()))
TN = (((0,), (0,)), ((), ()))
NT = (((1,), (1,)), ((), ()))


def mxu(a, b, dims):
    return lax.dot_general(a, b, dims, preferred_element_type=F32)


def pieces3(x):
    a = x.astype(BF16).astype(F32)
    r = x - a
    b = r.astype(BF16).astype(F32)
    c = r - b
    return a, b, c


def left_stack(x):
    a, b, c = pieces3(x)
    return jnp.concatenate([a, a, b, b, a, c], axis=0).astype(BF16)


def right_stack(x):
    a, b, c = pieces3(x)
    return jnp.concatenate([a, b, a, b, c, a], axis=0).astype(BF16)


def hi_lo_rows(x):
    hi = x.astype(BF16).astype(F32)
    return jnp.concatenate([hi, x - hi], axis=0).astype(BF16)


def twice(x):
    return jnp.concatenate([x, x], axis=1)


def row_fields(f_ref, i):
    block = f_ref[i >> 2, (i >> 1) & 1]
    return pltpu.roll(block, (i & 1) * ROWS, axis=1)[:, :ROWS]


def lane_fields(f_ref, j):
    return jnp.concatenate([f_ref[j, 0], f_ref[j, 1]], axis=1)


def distances(f_ref, pick, i, j):
    left = left_stack(row_fields(f_ref, i))
    lanes = lane_fields(f_ref, j)
    row = lax.broadcasted_iota(jnp.int32, (8, TILE), 0)
    norm = lanes[ROW_NORM : ROW_NORM + 1, :]
    right = jnp.where(row < 3, -2.0 * lanes, jnp.where(row == ROW_ONE, norm, jnp.where(row == ROW_NORM, 1.0, 0.0)))
    squared = mxu(left, right_stack(right), TN)
    return (squared,) if pick is None else (squared, mxu(left, pick, TN))


def lane_row(f_ref, j, which):
    return jnp.concatenate([f_ref[j, 0, which : which + 1, :], f_ref[j, 1, which : which + 1, :]], axis=1)


def fold_rows(x):
    total = x[0:8]
    for k in range(1, x.shape[0] // 8):
        total = total + x[8 * k : 8 * k + 8]
    return total


def add_lanes(out, j, values):
    out[j, 0] += values[:, :LANES]
    out[j, 1] += values[:, LANES:]


def add_rows(out, i, values):
    lane = lax.broadcasted_iota(jnp.int32, (8, LANES), 1)
    out[i >> 2, (i >> 1) & 1] += jnp.where((lane >> 6) == (i & 1), twice(values), 0.0)


def root(squared):
    squared = jnp.maximum(squared, TINY)
    return squared * lax.rsqrt(squared)


def density_self_values(parts, f_ref, i, j):
    squared, column = parts
    dist = root(squared)
    h = lane_row(f_ref, j, ROW_H)
    t = jnp.maximum(h - dist, 0.0)
    t = t * t
    return fold_rows(t * t * (h + 4.0 * dist) * twice(column))


def density_pair_values(parts, f_ref, i, j):
    squared, column = parts
    dist = root(squared)
    four = 4.0 * dist
    h_row, m_row = twice(column[:, :LANES]), twice(column[:, LANES:])
    h, m = lane_row(f_ref, j, ROW_H), lane_row(f_ref, j, ROW_MASS)
    t = jnp.maximum(h_row - dist, 0.0)
    t = t * t
    near = t * t * (h_row + four) * m
    s = jnp.maximum(h - dist, 0.0)
    s = s * s
    far = s * s * (h + four) * m_row
    return (*hi_lo(near[:, :LANES] + near[:, LANES:]), fold_rows(far))


def density_pair_store(values, out, i, j):
    hi, lo, far = values
    add_lanes(out, j, far)
    one = (lax.broadcasted_iota(jnp.int32, (16, LANES), 0) == 0).astype(BF16)
    add_rows(out, i, (mxu(one, hi, NT) + mxu(one, lo, NT))[0:8])


def hi_lo(x):
    hi = x.astype(BF16)
    return hi, (x - hi.astype(F32)).astype(BF16)


def force_values(parts, f_ref, i, j):
    squared, column = parts
    dist = root(squared)
    h_row, g_row = twice(column[:, :LANES]), twice(column[:, LANES:])
    h, g = lane_row(f_ref, j, ROW_H), lane_row(f_ref, j, ROW_G)
    a = jnp.maximum(h_row - dist, 0.0)
    b = jnp.maximum(h - dist, 0.0)
    return hi_lo(g_row * (a * a * a) + g * (b * b * b))


def moments(x):
    return hi_lo_rows(x * x[ROW_MASS : ROW_MASS + 1, :])


def force_self_values(parts, f_ref, i, j):
    b = jnp.maximum(lane_row(f_ref, j, ROW_H) - root(parts[0]), 0.0)
    return hi_lo(b * b * b)


def force_self_store(values, f_ref, out, i, j):
    hi, lo = values
    g = lane_row(f_ref, j, ROW_G)
    rows = moments(row_fields(f_ref, i))
    add_lanes(out, j, g * fold_rows(mxu(rows, hi, NN) + mxu(rows, lo, NN)))
    lanes = lane_fields(f_ref, j)
    lanes = hi_lo_rows(lanes * (lanes[ROW_MASS : ROW_MASS + 1, :] * g))
    add_rows(out, i, fold_rows(mxu(lanes, hi, NT) + mxu(lanes, lo, NT)))


def force_store(values, f_ref, out, i, j):
    hi, lo = values
    rows = moments(row_fields(f_ref, i))
    add_lanes(out, j, fold_rows(mxu(rows, hi, NN) + mxu(rows, lo, NN)))
    lanes = moments(lane_fields(f_ref, j))
    add_rows(out, i, fold_rows(mxu(lanes, hi, NT) + mxu(lanes, lo, NT)))


def sweep(unroll, lead, lag, count, units, slots, stage_a, stage_b, stage_c):
    part_slots, value_slots = slots

    def unit(index):
        code = units[index]
        return code >> 16, code & 0xFFFF

    def save(refs, k, values):
        for ref, value in zip(refs, values):
            ref[k] = value

    def restore(refs, k):
        return tuple(ref[k] for ref in refs)

    for ref in value_slots:
        ref[...] = jnp.zeros_like(ref)
    for k in range(lead):
        save(part_slots, k, stage_a(*unit(k)))

    def body(step, carry):
        base = step * unroll
        ids = [unit(base + k) for k in range(unroll + lead)]
        behind = [unit(jnp.maximum(base - lag + k, 0)) for k in range(lag)]
        parts = {k: restore(part_slots, k) for k in range(lead)}
        values = {k - lag: restore(value_slots, k) for k in range(lag)}
        for k in range(unroll):
            parts[k + lead] = stage_a(*ids[k + lead])
            values[k] = stage_b(parts.pop(k), *ids[k])
            stage_c(values.pop(k - lag), *(behind[k] if k < lag else ids[k - lag]))
        for k in range(lead):
            save(part_slots, k, parts[unroll + k])
        for k in range(lag):
            save(value_slots, k, values[unroll - lag + k])
        return carry

    lax.fori_loop(0, count, body, 0)
    for k in range(lag):
        stage_c(restore(value_slots, k), *unit(jnp.maximum(count * unroll - lag + k, 0)))


HANDED = {"density_self": (2, 1), "density": (2, 1), "force_self": (2, 2), "force": (2, 1)}


def slot_shapes(kind):
    lead, lag = HANDED[kind]
    parts = [pltpu.VMEM((lead, ROWS, TILE), F32)]
    if kind == "density_self":
        parts.append(pltpu.VMEM((lead, ROWS, LANES), F32))
    elif kind != "force_self":
        parts.append(pltpu.VMEM((lead, ROWS, TILE), F32))
    if kind == "density_self":
        values = [pltpu.VMEM((lag, 8, TILE), F32)]
    elif kind == "density":
        values = [pltpu.VMEM((lag, ROWS, LANES), BF16)] * 2 + [pltpu.VMEM((lag, 8, TILE), F32)]
    else:
        values = [pltpu.VMEM((lag, ROWS, TILE), BF16)] * 2
    return (parts, values)


def sweep_kind(kind, unroll, count, units, f_ref, pick, out, slots):
    picked = {"density_self": pick[:, LANES:], "force_self": None}.get(kind, pick[...])
    middle = {
        "density_self": lambda p, i, j: (density_self_values(p, f_ref, i, j),),
        "density": lambda p, i, j: density_pair_values(p, f_ref, i, j),
        "force_self": lambda p, i, j: force_self_values(p, f_ref, i, j),
        "force": lambda p, i, j: force_values(p, f_ref, i, j),
    }
    last = {
        "density_self": lambda v, i, j: add_lanes(out, j, v[0]),
        "density": lambda v, i, j: density_pair_store(v, out, i, j),
        "force_self": lambda v, i, j: force_self_store(v, f_ref, out, i, j),
        "force": lambda v, i, j: force_store(v, f_ref, out, i, j),
    }
    sweep(
        unroll, *HANDED[kind], count[0], units, slots,
        lambda i, j: distances(f_ref, picked, i, j), middle[kind], last[kind],
    )


def density_scale(h):
    h2 = h * h
    h4 = h2 * h2
    return KERNEL_NORM / (h4 * h4)


def each_group(cells, body):
    def step(k, carry):
        for half in range(2):
            body(pl.multiple_of(k * 8, 8), half)
        return carry

    lax.fori_loop(0, cells // 8, step, 0)


def half_lanes(half):
    return slice(half * LANES, (half + 1) * LANES)


def prepare_kernel(counts, targets, pos, smooth, masses, fields, outgoing, alive):
    cells = smooth.shape[0]
    fields[cells] = jnp.zeros((2, 8, LANES), F32)
    sub = lax.broadcasted_iota(jnp.int32, (8, LANES), 0)
    lane = lax.broadcasted_iota(jnp.int32, (8, LANES), 1)

    def group(c, half):
        count = jnp.zeros((8, LANES), jnp.int32)
        for k in range(8):
            count = jnp.where(sub == k, counts[c + k], count)
        at = (pl.ds(c, 8), half_lanes(half))
        x, y, z = (pos[k, at[0], at[1]] - 0.5 for k in range(3))
        live = lane + half * LANES < count
        alive[at] = jnp.where(live, 1.0, 0.0)
        mass = jnp.where(live, masses[at], 0.0)
        rows = (x, y, z, x * x + y * y + z * z, jnp.ones_like(x), smooth[at], mass, count.astype(F32))
        for k in range(8):
            fields[pl.ds(c, 8), half, k, :] = rows[k]

    each_group(cells, group)

    def export(k, carry):
        for s in range(8):
            slot = k * 8 + s
            outgoing[slot] = fields[jnp.maximum(targets[slot], 0)]
        return carry

    lax.fori_loop(0, outgoing.shape[0] // 8, export, 0)


def load_fields(sources, f_ref, acc, sems):
    copies, first = [], 0
    for k, source in enumerate(sources):
        copies.append(pltpu.make_async_copy(source, f_ref.at[pl.ds(first, source.shape[0])], sems.at[k]))
        first += source.shape[0]
    for copy in copies:
        copy.start()
    acc[...] = jnp.zeros_like(acc)
    for copy in copies:
        copy.wait()


def density_inner_kernel(kind, unroll, count, units, own, pick, out, f_ref, acc, sems, *slots):
    load_fields([own], f_ref, acc, sems)
    sweep_kind(kind, unroll, count, units, f_ref, pick, acc, slots)

    def finish(c, half):
        out[pl.ds(c, 8), half_lanes(half)] = jnp.sum(acc[pl.ds(c, 8), half], axis=1)

    each_group(out.shape[0], finish)


def density_outer_kernel(unroll, count, units, own, ghosts, pick, own_out, ghost_out, f_ref, acc, sems, *slots):
    load_fields([own, ghosts], f_ref, acc, sems)
    sweep_kind("density", unroll, count, units, f_ref, pick, acc, slots)
    first = own.shape[0]

    def finish_own(c, half):
        own_out[pl.ds(c, 8), half_lanes(half)] = jnp.sum(acc[pl.ds(c, 8), half], axis=1)

    def finish_ghost(c, half):
        total = jnp.sum(acc[pl.ds(first + c, 8), half], axis=1)
        scale = density_scale(f_ref[pl.ds(first + c, 8), half, ROW_H, :])
        ghost_out[pl.ds(c, 8), 0, half_lanes(half)] = total * scale

    each_group(own_out.shape[0], finish_own)
    each_group(ghost_out.shape[0], finish_ghost)


def select(targets, cells):
    ids = lax.broadcasted_iota(jnp.int32, (cells, targets.shape[1]), 0)
    return (ids == targets[...]).astype(BF16)


def exact_dot(selector, values, dims):
    a, b, c = (x.astype(BF16) for x in pieces3(values))
    return mxu(selector, a, dims) + mxu(selector, b, dims) + mxu(selector, c, dims)


def factor_kernel(targets, self_rho, inner, outer, returned, alive, smooth, entropy, density, g_out, outgoing):
    cells = density.shape[0]
    selector = select(targets, cells)
    live = alive[...] > 0.0
    scale = density_scale(smooth[...])
    total = (self_rho[...] + inner[...] + outer[...]) * scale + exact_dot(selector, returned[:, 0, :], NN)
    rho = jnp.where(live, total, 0.0)
    density[...] = rho
    safe = jnp.where(live, rho, 1.0)
    g = jnp.where(live, entropy[...] * jnp.exp(jnp.log(safe) * (-1.0 / 3.0)) * (20.0 * scale), 0.0)
    g_out[...] = g
    outgoing[:, 0, :] = exact_dot(selector, g, TN)


def insert_g(f_ref, g, first, load):
    def body(c, half):
        f_ref[pl.ds(first + c, 8), half, ROW_G, :] = load(g, c, half)

    each_group(g.shape[0], body)


def natural(g, c, half):
    return g[pl.ds(c, 8), half_lanes(half)]


def by_slot(g, c, half):
    return g[pl.ds(c, 8), 0, half_lanes(half)]


def finish_force(f_ref, acc, out):
    def body(c, half):
        def row(ref, k):
            return ref[pl.ds(c, 8), half, k, :]

        live = row(f_ref, ROW_MASS) > 0.0
        total = row(acc, ROW_ONE)
        for k in range(3):
            out[k, pl.ds(c, 8), half_lanes(half)] = jnp.where(live, row(f_ref, k) * total - row(acc, k), 0.0)

    each_group(out.shape[1], body)


def force_inner_kernel(kind, unroll, count, units, own, own_g, pick, out, f_ref, acc, sems, *slots):
    load_fields([own], f_ref, acc, sems)
    insert_g(f_ref, own_g, 0, natural)
    sweep_kind(kind, unroll, count, units, f_ref, pick, acc, slots)
    finish_force(f_ref, acc, out)


def force_outer_kernel(unroll, count, units, own, ghosts, own_g, ghost_g, pick, own_out, ghost_out, f_ref, acc, sems, *slots):
    load_fields([own, ghosts], f_ref, acc, sems)
    first = own.shape[0]
    insert_g(f_ref, own_g, 0, natural)
    insert_g(f_ref, ghost_g, first, by_slot)
    sweep_kind("force", unroll, count, units, f_ref, pick, acc, slots)
    finish_force(f_ref, acc, own_out)

    def finish(k, carry):
        for s in range(4):
            for half in range(2):
                f, sums = f_ref[first + 4 * k + s, half], acc[first + 4 * k + s, half]
                live = f[ROW_MASS : ROW_MASS + 1, :] > 0.0
                ghost_out[4 * k + s, half] = jnp.where(live, f * sums[ROW_ONE : ROW_ONE + 1, :] - sums, 0.0)[0:4]
        return carry

    lax.fori_loop(0, ghost_out.shape[0] // 4, finish, 0)


def final_kernel(targets, self_acc, inner_acc, outer_acc, returned, acceleration):
    selector = select(targets, acceleration.shape[1])
    for half in range(2):
        lanes = half_lanes(half)
        for k in range(3):
            here = self_acc[k, :, lanes] + inner_acc[k, :, lanes] + outer_acc[k, :, lanes]
            acceleration[k, :, lanes] = here + exact_dot(selector, returned[:, half, k, :], NN)


SMEM = pl.BlockSpec(memory_space=pltpu.SMEM)
VMEM = pl.BlockSpec(memory_space=pltpu.VMEM)
ANY = pl.BlockSpec(memory_space=pl.ANY)


def launch(body, name, in_specs, shapes, args, scratch=(), flops=0, limit=40):
    return pl.pallas_call(
        body,
        out_shape=[jax.ShapeDtypeStruct(shape, F32) for shape in shapes],
        in_specs=in_specs,
        out_specs=[VMEM] * len(shapes),
        scratch_shapes=list(scratch),
        name=name,
        compiler_params=pltpu.CompilerParams(vmem_limit_bytes=limit * 1024 * 1024),
        cost_estimate=pl.CostEstimate(flops=flops, bytes_accessed=1 << 21, transcendentals=0),
    )(*args)


def pick_matrix(second):
    k = lax.broadcasted_iota(jnp.int32, (48, TILE), 0)
    lane = lax.broadcasted_iota(jnp.int32, (48, TILE), 1)
    group, row = k // 8, k % 8
    used = (group == 0) | (group == 2) | (group == 5)
    return (used & (row == jnp.where(lane < LANES, ROW_H, second))).astype(BF16)


def compact(valid, code, spare, unroll):
    num = valid.shape[0]
    flags = valid.astype(jnp.int32)
    ids = jnp.arange(num, dtype=jnp.int32)
    rank = jnp.sum(jnp.where(ids[None, :] < ids[:, None], flags[None, :], 0), axis=1)
    total = jnp.sum(flags)
    hit = (rank[None, :] == ids[:, None]) & valid[None, :]
    listed = jnp.sum(jnp.where(hit, code[None, :], 0), axis=1)
    listed = jnp.where(ids < total, listed, spare)
    listed = jnp.concatenate([listed, jnp.full((LANES,), spare, listed.dtype)])
    return listed.astype(jnp.int32), ((total + unroll - 1) // unroll).reshape(1).astype(jnp.int32)


def look_up(table, ids):
    slots = jnp.arange(table.shape[0], dtype=jnp.int32)
    return jnp.sum(jnp.where(ids[:, None] == slots[None, :], table[None, :], 0), axis=1)


def pair_units(first, second, live, counts, spare, unroll):
    n_first, n_second = look_up(counts, first), look_up(counts, second)
    swap = n_second < n_first
    rows = jnp.where(swap, second, first)
    lanes = jnp.where(swap, first, second)
    chunks = (jnp.minimum(n_first, n_second) + ROWS - 1) // ROWS
    step = jnp.arange(CHUNKS, dtype=jnp.int32)
    valid = (step[None, :] < chunks[:, None]) & live[:, None]
    code = ((rows[:, None] * CHUNKS + step[None, :]) << 16) | lanes[:, None]
    return compact(valid.reshape(-1), code.reshape(-1), spare, unroll)


def trade(payload):
    return lax.all_to_all(payload, AXES, split_axis=0, concat_axis=0, tiled=True)


def local(positions, smooth, masses, entropy, cell_counts, cell_pairs, pair_count, send_cells):
    cells, tile = smooth.shape
    num_pairs = cell_pairs.shape[1]
    slots = send_cells.shape[1]
    unroll = 32
    targets = send_cells[0]
    padded = (cells + 1, 2, 8, LANES)
    whole = (cells + 1 + slots, 2, 8, LANES)
    pick_m, pick_g = pick_matrix(ROW_MASS), pick_matrix(ROW_G)
    spare = ((cells * CHUNKS) << 16) | cells
    unit = ROWS * TILE * 2000
    both_sems = pltpu.SemaphoreType.DMA((2,))

    own, outgoing, alive = launch(
        prepare_kernel, "prepare", [SMEM, SMEM, VMEM, VMEM, VMEM], [padded, (slots, 2, 8, LANES), (cells, tile)],
        (cell_counts, targets, positions, smooth, masses),
    )
    ghosts = trade(outgoing)

    step = jnp.arange(CHUNKS, dtype=jnp.int32)
    ids = jnp.arange(cells, dtype=jnp.int32)
    self_valid = step[None, :] < ((cell_counts + ROWS - 1) // ROWS)[:, None]
    self_code = ((ids[:, None] * CHUNKS + step[None, :]) << 16) | ids[:, None]
    self_units, self_count = compact(self_valid.reshape(-1), self_code.reshape(-1), spare, unroll)
    live_pair = jnp.arange(num_pairs, dtype=jnp.int32) < pair_count[0]
    first, second = cell_pairs[0], cell_pairs[1]
    second = jnp.where(second < cells, second, second + 1)
    inner_units, inner_count = pair_units(first[slots:], second[slots:], live_pair[slots:], cell_counts, spare, unroll)

    def scratch(shape, kind):
        return [pltpu.VMEM(shape, F32), pltpu.VMEM(shape, F32), both_sems, *slot_shapes(kind)]

    (self_rho,) = launch(
        functools.partial(density_inner_kernel, "density_self", unroll), "density_self", [SMEM, SMEM, ANY, VMEM],
        [(cells, tile)], (self_count, self_units, own, pick_m), scratch(padded, "density_self"), 768 * unit,
    )
    ghosts, self_rho = lax.optimization_barrier((ghosts, self_rho))

    ghost_counts = jnp.max(ghosts[:, 0, ROW_G, :], axis=-1).astype(jnp.int32)
    all_counts = jnp.concatenate([cell_counts, jnp.zeros((1,), jnp.int32), ghost_counts])
    outer_units, outer_count = pair_units(first[:slots], second[:slots], live_pair[:slots], all_counts, spare, unroll)
    outer_rho, ghost_rho = launch(
        functools.partial(density_outer_kernel, unroll), "density_outer", [SMEM, SMEM, ANY, ANY, VMEM],
        [(cells, tile), (slots, 1, tile)], (outer_count, outer_units, own, ghosts, pick_m),
        scratch(whole, "density"), 640 * unit,
    )
    returned_rho = trade(ghost_rho)
    (inner_rho,) = launch(
        functools.partial(density_inner_kernel, "density", unroll), "density_inner", [SMEM, SMEM, ANY, VMEM],
        [(cells, tile)], (inner_count, inner_units, own, pick_m), scratch(padded, "density"), 320 * unit,
    )
    returned_rho, inner_rho = lax.optimization_barrier((returned_rho, inner_rho))

    density, own_g, outgoing_g = launch(
        factor_kernel, "factor", [VMEM] * 8, [(cells, tile), (cells, tile), (slots, 1, tile)],
        (send_cells, self_rho, inner_rho, outer_rho, returned_rho, alive, smooth, entropy),
    )
    ghost_g = trade(outgoing_g)
    (self_acc,) = launch(
        functools.partial(force_inner_kernel, "force_self", unroll), "force_self", [SMEM, SMEM, ANY, VMEM, VMEM],
        [(3, cells, tile)], (self_count, self_units, own, own_g, pick_g), scratch(padded, "force_self"), 768 * unit,
    )
    ghost_g, self_acc = lax.optimization_barrier((ghost_g, self_acc))

    outer_acc, ghost_acc = launch(
        functools.partial(force_outer_kernel, unroll), "force_outer", [SMEM, SMEM, ANY, ANY, VMEM, VMEM, VMEM],
        [(3, cells, tile), (slots, 2, 4, LANES)], (outer_count, outer_units, own, ghosts, own_g, ghost_g, pick_g),
        scratch(whole, "force"), 640 * unit,
    )
    returned_acc = trade(ghost_acc)
    (inner_acc,) = launch(
        functools.partial(force_inner_kernel, "force", unroll), "force_inner", [SMEM, SMEM, ANY, VMEM, VMEM],
        [(3, cells, tile)], (inner_count, inner_units, own, own_g, pick_g), scratch(padded, "force"), 320 * unit,
    )
    returned_acc, inner_acc = lax.optimization_barrier((returned_acc, inner_acc))

    (acceleration,) = launch(
        final_kernel, "final", [VMEM] * 5, [(3, cells, tile)],
        (send_cells, self_acc, inner_acc, outer_acc, returned_acc),
    )
    return (density, acceleration)


def solution(mesh):
    in_specs = (
        P(None, AXES, None),
        P(AXES, None),
        P(AXES, None),
        P(AXES, None),
        P(AXES),
        P(None, AXES),
        P(AXES),
        P(AXES, None),
    )
    out_specs = (P(AXES, None), P(None, AXES, None))
    return jax.shard_map(local, mesh=mesh, in_specs=in_specs, out_specs=out_specs, check_vma=False)
```

time: 332 us -> 316 us (0.952)
  the two profiles are of different devices: /device:TPU:1 before, /device:TPU:14 now
where the time goes in v3:
time: 316 us; the launch traced here: 313 us
  Pallas kernels  221 us (70%)
  starting transfers between devices  51.7 us (16%)
  local copies, waits for them, and re-layouts  27 us (9%)
  other arithmetic  9.17 us (3%)
  between operations  3.84 us (1%)
    pallas_call x9, Pallas kernels, launch(): pl.pallas_call(body, out_shape=[jax.ShapeDtypeStruct(shape, F32) for shap...  221 us
    all_to_all x4, starting transfers between devices, trade(): lax.all_to_all(payload, AXES, split_axis=0, concat_axis=0, tiled=True)  51.7 us
    unnamed x58, local copies, waits for them, and re-layouts  26.2 us
  transfers between devices with their start and end apart: 4, of which 0 were waited for; matrix products, arithmetic and copies ran while one was open for 2% of the time, Pallas kernels for 39%

profile of v3, /device:TPU:14, one launch (start us, length us, event | category | flops | bytes accessed | tf_op | source)
XLA Modules:
  0.0 313.0 jit_solution(5134260129135970263)
XLA Ops:
  1.6 1.1 copy-done.7
  5.0 2.6 prepare.1
  7.6 1.3 copy-done
  8.9 1.4 copy-done.19
  10.3 10.4 %all-to-all-start = ((f32[256,2,8,128]{3,2,1,0:T(8,128)}), f32[256,2,8,128]{3,2,1,0:T(8,128)S(1)}, u32[]{:S(2)}, u32[]{:S(2)}) async-start(f32[256,2,8,128]{3,2,1,0:T(8,128)} %copy-done), calls=%async_computation | async-start | bytes 4194304 | tf_op jit(solution)/shard_map/all_to_all | solution.py:488
  28.4 1.6 copy-done.20
  30.0 34.2 %density_self.1.self_rho = f32[256,256]{1,0:T(8,128)S(1)} custom-call(s32[1]{0:T(128)} %bitcast.1.count, s32[1152]{0:T(1024)S(1)} %concatenate.12.units, f32[257,2,8,128]{3,2,1,0:T(8,128)S(1)} %copy-done.20, bf16[48,256]{1,0:T(8,128)(2,1)S(1)} %get-tuple-element.47.pick), custom_call_target="tpu_custom_call" | custom-call | flops 25165824000 | bytes 2097152 | tf_op jit(solution)/shard_map/density_self/pallas_call | solution.py:437
  69.4 1.6 copy-done.21
  71.0 46.4 %density_outer.1 = (f32[256,256]{1,0:T(8,128)S(1)}, f32[256,1,256]{2,1,0:T(1,128)}) custom-call(s32[1]{0:T(128)} %bitcast.4.count, s32[1152]{0:T(1024)S(1)} %concatenate.14.units, f32[257,2,8,128]{3,2,1,0:T(8,128)S(1)} %copy-done.21, f32[256,2,8,128]{3,2,1,0:T(8,128)S(1)} %all-to-all-done.ghosts, bf16[48,256]{1,0:T(8,128)(2,1)S(1)} %get-tuple-element.47.pick), custom_call_target="tpu_custom_call" | custom-call | flops 20971520000 | bytes 2097152 | tf_op jit(solution)/shard_map/density_outer/pallas_call | solution.py:437
  118.1 14.9 %all-to-all-start.1 = ((f32[256,1,256]{2,1,0:T(1,128)}), f32[256,1,256]{2,1,0:T(1,128)S(1)}, u32[]{:S(2)}, u32[]{:S(2)}) async-start(f32[256,1,256]{2,1,0:T(1,128)} %get-tuple-element.24), calls=%async_computation.1 | async-start | bytes 524288 | tf_op jit(solution)/shard_map/all_to_all | solution.py:488
  133.0 1.6 copy-done.22
  134.6 23.3 %density_inner.1.inner = f32[256,256]{1,0:T(8,128)S(1)} custom-call(s32[1]{0:T(128)} %bitcast.6.count, s32[640]{0:T(1024)S(1)} %concatenate.15.units, f32[257,2,8,128]{3,2,1,0:T(8,128)S(1)} %copy-done.22, bf16[48,256]{1,0:T(8,128)(2,1)S(1)} %get-tuple-element.47.pick), custom_call_target="tpu_custom_call" | custom-call | flops 10485760000 | bytes 2097152 | tf_op jit(solution)/shard_map/density_inner/pallas_call | solution.py:437
  160.6 2.4 factor.1
  164.4 11.6 %all-to-all-start.2 = ((f32[256,1,256]{2,1,0:T(1,128)}), f32[256,1,256]{2,1,0:T(1,128)S(1)}, u32[]{:S(2)}, u32[]{:S(2)}) async-start(f32[256,1,256]{2,1,0:T(1,128)} %copy-done.14), calls=%async_computation.2 | async-start | bytes 524288 | tf_op jit(solution)/shard_map/all_to_all | solution.py:488
  176.1 1.6 copy-done.23
  178.6 44.0 %force_self.1.self_acc = f32[3,256,256]{2,1,0:T(8,128)S(1)} custom-call(s32[1]{0:T(128)} %bitcast.1.count, s32[1152]{0:T(1024)S(1)} %concatenate.12.units, f32[257,2,8,128]{3,2,1,0:T(8,128)S(1)} %copy-done.23, f32[256,256]{1,0:T(8,128)S(1)} %copy-done.27, bf16[48,256]{1,0:T(8,128)(2,1)S(1)} %get-tuple-element.46.pick), custom_call_target="tpu_custom_call" | custom-call | flops 25165824000 | bytes 2097152 | tf_op jit(solution)/shard_map/force_self/pallas_call | solution.py:437
  222.6 1.6 copy-done.24
  224.2 42.0 %force_outer.1 = (f32[3,256,256]{2,1,0:T(8,128)S(1)}, f32[256,2,4,128]{3,2,1,0:T(4,128)}) custom-call(s32[1]{0:T(128)} %bitcast.4.count, s32[1152]{0:T(1024)S(1)} %concatenate.14.units, f32[257,2,8,128]{3,2,1,0:T(8,128)S(1)} %copy-done.24, f32[256,2,8,128]{3,2,1,0:T(8,128)S(1)} %all-to-all-done.ghosts, f32[256,256]{1,0:T(8,128)S(1)} %copy-done.27, ...), custom_call_target="tpu_custom_call" | custom-call | flops 20971520000 | bytes 2097152 | tf_op jit(solution)/shard_map/force_outer/pallas_call | solution.py:437
  267.1 14.8 %all-to-all-start.3 = ((f32[256,2,4,128]{3,2,1,0:T(4,128)}), f32[256,2,4,128]{3,2,1,0:T(4,128)S(1)}, u32[]{:S(2)}, u32[]{:S(2)}) async-start(f32[256,2,4,128]{3,2,1,0:T(4,128)} %get-tuple-element.34), calls=%async_computation.3 | async-start | bytes 2097152 | tf_op jit(solution)/shard_map/all_to_all | solution.py:488
  281.9 1.6 copy-done.25
  283.5 21.5 %force_inner.1.inner_acc = f32[3,256,256]{2,1,0:T(8,128)S(1)} custom-call(s32[1]{0:T(128)} %bitcast.6.count, s32[640]{0:T(1024)S(1)} %concatenate.15.units, f32[257,2,8,128]{3,2,1,0:T(8,128)S(1)} %copy-done.25, f32[256,256]{1,0:T(8,128)S(1)} %copy-done.27, bf16[48,256]{1,0:T(8,128)(2,1)S(1)} %get-tuple-element.46.pick), custom_call_target="tpu_custom_call" | custom-call | flops 10485760000 | bytes 2097152 | tf_op jit(solution)/shard_map/force_inner/pallas_call | solution.py:437
  305.9 1.1 copy-done.4
  307.0 1.1 copy-done.6
  308.2 4.8 %final.1 = f32[3,256,256]{2,1,0:T(8,128)} custom-call(s32[1,256]{1,0:T(1,128)S(1)} %copy-done.18, f32[3,256,256]{2,1,0:T(8,128)S(1)} %force_self.1.self_acc, f32[3,256,256]{2,1,0:T(8,128)S(1)} %copy-done.6, f32[3,256,256]{2,1,0:T(8,128)S(1)} %copy-done.4, f32[256,2,4,128]{3,2,1,0:T(4,128)S(1)} %all-to-all-done.3.returned), custom_call_target="tpu_custom_call" | custom-call | bytes 2097152 | tf_op jit(solution)/shard_map/final/pallas_call | solution.py:437
  (103 shorter events, 20.6 us)
Async XLA Ops:
  0.6 1.0 copy-start.1
  1.6 1.1 copy-start.7
  2.7 0.9 copy-start.8
  7.6 1.3 copy-start
  8.9 1.4 copy-start.19
  10.3 10.4 %copy-start.16 = (s32[256]{0:T(256)S(1)}, s32[256]{0:T(256)}, u32[]{:S(2)}) copy-start(s32[256]{0:T(256)} %counts.1) | copy-start | bytes 3076
  10.3 12.0 %copy-start.28 = (s32[2,384]{1,0:T(2,128)S(1)}, s32[2,384]{1,0:T(2,128)}, u32[]{:S(2)}) copy-start(s32[2,384]{1,0:T(2,128)} %param.13) | copy-start | bytes 9220
  10.3 53.9 %all-to-all-start = ((f32[256,2,8,128]{3,2,1,0:T(8,128)}), f32[256,2,8,128]{3,2,1,0:T(8,128)S(1)}, u32[]{:S(2)}, u32[]{:S(2)}) async-start(f32[256,2,8,128]{3,2,1,0:T(8,128)} %copy-done), calls=%async_computation | async-start | bytes 4194304 | tf_op jit(solution)/shard_map/all_to_all | solution.py:488
  28.4 1.6 copy-start.20
  69.4 1.6 copy-start.21
  118.1 40.6 %all-to-all-start.1 = ((f32[256,1,256]{2,1,0:T(1,128)}), f32[256,1,256]{2,1,0:T(1,128)S(1)}, u32[]{:S(2)}, u32[]{:S(2)}) async-start(f32[256,1,256]{2,1,0:T(1,128)} %get-tuple-element.24), calls=%async_computation.1 | async-start | bytes 524288 | tf_op jit(solution)/shard_map/all_to_all | solution.py:488
  133.0 1.6 copy-start.22
  134.6 24.1 %copy-start.2 = (f32[256,256]{1,0:T(8,128)S(1)}, f32[256,256]{1,0:T(8,128)}, u32[]{:S(2)}) copy-start(f32[256,256]{1,0:T(8,128)} %smooth.3) | copy-start | bytes 786436
  134.6 24.1 %copy-start.9 = (f32[256,256]{1,0:T(8,128)S(1)}, f32[256,256]{1,0:T(8,128)}, u32[]{:S(2)}) copy-start(f32[256,256]{1,0:T(8,128)} %entropy.1) | copy-start | bytes 786436
  134.6 24.1 %copy-start.18 = (s32[1,256]{1,0:T(1,128)S(1)}, s32[1,256]{1,0:T(1,128)}, u32[]{:S(2)}) copy-start(s32[1,256]{1,0:T(1,128)} %targets.3) | copy-start | bytes 3076
  158.7 1.0 copy-start.11
  159.7 0.9 copy-start.13
  164.4 58.2 %all-to-all-start.2 = ((f32[256,1,256]{2,1,0:T(1,128)}), f32[256,1,256]{2,1,0:T(1,128)S(1)}, u32[]{:S(2)}, u32[]{:S(2)}) async-start(f32[256,1,256]{2,1,0:T(1,128)} %copy-done.14), calls=%async_computation.2 | async-start | bytes 524288 | tf_op jit(solution)/shard_map/all_to_all | solution.py:488
  176.0 1.6 copy-start.23
  222.6 1.6 copy-start.24
  267.1 38.8 %all-to-all-start.3 = ((f32[256,2,4,128]{3,2,1,0:T(4,128)}), f32[256,2,4,128]{3,2,1,0:T(4,128)S(1)}, u32[]{:S(2)}, u32[]{:S(2)}) async-start(f32[256,2,4,128]{3,2,1,0:T(4,128)} %get-tuple-element.34), calls=%async_computation.3 | async-start | bytes 2097152 | tf_op jit(solution)/shard_map/all_to_all | solution.py:488
  281.9 1.6 copy-start.25
  305.9 1.1 copy-start.4
  307.0 1.1 copy-start.6
  (9 other events, 6.9 us)

commit v4 on v3

--- a/solution.py
+++ b/solution.py
@@ -70,7 +70,7 @@
     lanes = lane_fields(f_ref, j)
     row = lax.broadcasted_iota(jnp.int32, (8, TILE), 0)
     norm = lanes[ROW_NORM : ROW_NORM + 1, :]
-    right = jnp.where(row < 3, -2.0 * lanes, jnp.where(row == ROW_ONE, norm, jnp.where(row == ROW_NORM, 1.0, 0.0)))
+    right = jnp.where(row < 3, -32.0 * lanes, jnp.where(row == ROW_ONE, 16.0 * norm, jnp.where(row == ROW_NORM, 16.0, 0.0)))
     squared = mxu(left, right_stack(right), TN)
     return (squared,) if pick is None else (squared, mxu(left, pick, TN))
 
@@ -105,23 +105,23 @@
     squared, column = parts
     dist = root(squared)
     h = lane_row(f_ref, j, ROW_H)
-    t = jnp.maximum(h - dist, 0.0)
+    t = jnp.maximum(4.0 * h - dist, 0.0)
     t = t * t
-    return fold_rows(t * t * (h + 4.0 * dist) * twice(column))
+    return fold_rows(t * t * (h + dist) * twice(column))
 
 
 def density_pair_values(parts, f_ref, i, j):
     squared, column = parts
     dist = root(squared)
-    four = 4.0 * dist
     h_row, m_row = twice(column[:, :LANES]), twice(column[:, LANES:])
+    quarter = twice(0.25 * column[:, :LANES])
     h, m = lane_row(f_ref, j, ROW_H), lane_row(f_ref, j, ROW_MASS)
     t = jnp.maximum(h_row - dist, 0.0)
     t = t * t
-    near = t * t * (h_row + four) * m
-    s = jnp.maximum(h - dist, 0.0)
+    near = t * t * (quarter + dist) * m
+    s = jnp.maximum(4.0 * h - dist, 0.0)
     s = s * s
-    far = s * s * (h + four) * m_row
+    far = s * s * (h + dist) * m_row
     return (*hi_lo(near[:, :LANES] + near[:, LANES:]), fold_rows(far))
 
 
@@ -143,7 +143,7 @@
     h_row, g_row = twice(column[:, :LANES]), twice(column[:, LANES:])
     h, g = lane_row(f_ref, j, ROW_H), lane_row(f_ref, j, ROW_G)
     a = jnp.maximum(h_row - dist, 0.0)
-    b = jnp.maximum(h - dist, 0.0)
+    b = jnp.maximum(4.0 * h - dist, 0.0)
     return hi_lo(g_row * (a * a * a) + g * (b * b * b))
 
 
@@ -152,7 +152,7 @@
 
 
 def force_self_values(parts, f_ref, i, j):
-    b = jnp.maximum(lane_row(f_ref, j, ROW_H) - root(parts[0]), 0.0)
+    b = jnp.maximum(4.0 * lane_row(f_ref, j, ROW_H) - root(parts[0]), 0.0)
     return hi_lo(b * b * b)
 
 
@@ -256,7 +256,7 @@
 def density_scale(h):
     h2 = h * h
     h4 = h2 * h2
-    return KERNEL_NORM / (h4 * h4)
+    return KERNEL_NORM / 256.0 / (h4 * h4)
 
 
 def each_group(cells, body):
@@ -314,8 +314,8 @@
         copy.wait()
 
 
-def density_inner_kernel(kind, unroll, count, units, own, pick, out, f_ref, acc, sems, *slots):
-    load_fields([own], f_ref, acc, sems)
+def density_inner_kernel(kind, unroll, count, units, f_ref, pick, out, acc, *slots):
+    acc[...] = jnp.zeros_like(acc)
     sweep_kind(kind, unroll, count, units, f_ref, pick, acc, slots)
 
     def finish(c, half):
@@ -360,7 +360,7 @@
     rho = jnp.where(live, total, 0.0)
     density[...] = rho
     safe = jnp.where(live, rho, 1.0)
-    g = jnp.where(live, entropy[...] * jnp.exp(jnp.log(safe) * (-1.0 / 3.0)) * (20.0 * scale), 0.0)
+    g = jnp.where(live, entropy[...] * jnp.exp(jnp.log(safe) * (-1.0 / 3.0)) * (80.0 * scale), 0.0)
     g_out[...] = g
     outgoing[:, 0, :] = exact_dot(selector, g, TN)
 
@@ -451,7 +451,8 @@
     lane = lax.broadcasted_iota(jnp.int32, (48, TILE), 1)
     group, row = k // 8, k % 8
     used = (group == 0) | (group == 2) | (group == 5)
-    return (used & (row == jnp.where(lane < LANES, ROW_H, second))).astype(BF16)
+    weight = jnp.where(lane < LANES, 4.0, 1.0)
+    return jnp.where(used & (row == jnp.where(lane < LANES, ROW_H, second)), weight, 0.0).astype(BF16)
 
 
 def compact(valid, code, spare, unroll):
@@ -485,7 +486,9 @@
 
 
 def trade(payload):
-    return lax.all_to_all(payload, AXES, split_axis=0, concat_axis=0, tiled=True)
+    peers = lax.axis_size(AXES)
+    by_peer = payload.reshape(peers, -1, *payload.shape[2:-1], LANES)
+    return lax.all_to_all(by_peer, AXES, split_axis=0, concat_axis=0, tiled=True).reshape(payload.shape)
 
 
 def local(positions, smooth, masses, entropy, cell_counts, cell_pairs, pair_count, send_cells):
@@ -521,8 +524,8 @@
         return [pltpu.VMEM(shape, F32), pltpu.VMEM(shape, F32), both_sems, *slot_shapes(kind)]
 
     (self_rho,) = launch(
-        functools.partial(density_inner_kernel, "density_self", unroll), "density_self", [SMEM, SMEM, ANY, VMEM],
-        [(cells, tile)], (self_count, self_units, own, pick_m), scratch(padded, "density_self"), 768 * unit,
+        functools.partial(density_inner_kernel, "density_self", unroll), "density_self", [SMEM, SMEM, VMEM, VMEM],
+        [(cells, tile)], (self_count, self_units, own, pick_m), [pltpu.VMEM(padded, F32), *slot_shapes("density_self")], 768 * unit,
     )
     ghosts, self_rho = lax.optimization_barrier((ghosts, self_rho))
 
@@ -536,8 +539,8 @@
     )
     returned_rho = trade(ghost_rho)
     (inner_rho,) = launch(
-        functools.partial(density_inner_kernel, "density", unroll), "density_inner", [SMEM, SMEM, ANY, VMEM],
-        [(cells, tile)], (inner_count, inner_units, own, pick_m), scratch(padded, "density"), 320 * unit,
+        functools.partial(density_inner_kernel, "density", unroll), "density_inner", [SMEM, SMEM, VMEM, VMEM],
+        [(cells, tile)], (inner_count, inner_units, own, pick_m), [pltpu.VMEM(padded, F32), *slot_shapes("density")], 320 * unit,
     )
     returned_rho, inner_rho = lax.optimization_barrier((returned_rho, inner_rho))
 

time: 316 us -> 310 us (0.981)
  the two profiles are of different devices: /device:TPU:14 before, /device:TPU:1 now
where the time goes in v4:
time: 310 us; the launch traced here: 307 us
  Pallas kernels  217 us (70%)
  starting transfers between devices  49.5 us (16%)
  local copies, waits for them, and re-layouts  27 us (9%)
  other arithmetic  9.18 us (3%)
  between operations  3.84 us (1%)
    pallas_call x9, Pallas kernels, launch(): pl.pallas_call(body, out_shape=[jax.ShapeDtypeStruct(shape, F32) for shap...  217 us
    all_to_all x4, starting transfers between devices, trade(): lax.all_to_all(by_peer, AXES, split_axis=0, concat_axis=0, tiled=True)  49.5 us
    unnamed x58, local copies, waits for them, and re-layouts  26.2 us
  transfers between devices with their start and end apart: 4, of which 0 were waited for; matrix products, arithmetic and copies ran while one was open for 2% of the time, Pallas kernels for 39%

profile of v4, /device:TPU:1, one launch (start us, length us, event | category | flops | bytes accessed | tf_op | source)
XLA Modules:
  0.0 306.9 jit_solution(3400809851518903469)
XLA Ops:
  1.6 1.1 copy-done.7
  5.0 2.6 prepare.1
  7.6 1.3 copy-done
  8.9 1.4 copy-done.19
  10.3 11.5 %all-to-all-start = ((f32[128,4,8,128]{3,2,1,0:T(8,128)}), f32[128,4,8,128]{3,2,1,0:T(8,128)S(1)}, u32[]{:S(2)}, u32[]{:S(2)}) async-start(f32[128,4,8,128]{3,2,1,0:T(8,128)} %bitcast.26), calls=%async_computation | async-start | bytes 4194304 | tf_op jit(solution)/shard_map/all_to_all | solution.py:491
  29.6 1.6 copy-done.20
  31.2 34.2 %density_self.1.self_rho = f32[256,256]{1,0:T(8,128)S(1)} custom-call(s32[1]{0:T(128)} %bitcast.3.count, s32[1152]{0:T(1024)S(1)} %concatenate.12.units, f32[257,2,8,128]{3,2,1,0:T(8,128)S(1)} %copy-done.20, bf16[48,256]{1,0:T(8,128)(2,1)S(1)} %get-tuple-element.47.pick), custom_call_target="tpu_custom_call" | custom-call | flops 25165824000 | bytes 2097152 | tf_op jit(solution)/shard_map/density_self/pallas_call | solution.py:437
  70.6 1.6 copy-done.21
  72.2 45.2 %density_outer.1 = (f32[256,256]{1,0:T(8,128)S(1)}, f32[256,1,256]{2,1,0:T(1,128)}) custom-call(s32[1]{0:T(128)} %bitcast.6.count, s32[1152]{0:T(1024)S(1)} %concatenate.14.units, f32[257,2,8,128]{3,2,1,0:T(8,128)S(1)} %copy-done.21, f32[256,2,8,128]{3,2,1,0:T(8,128)S(1)} %bitcast.24, bf16[48,256]{1,0:T(8,128)(2,1)S(1)} %get-tuple-element.47.pick), custom_call_target="tpu_custom_call" | custom-call | flops 20971520000 | bytes 2097152 | tf_op jit(solution)/shard_map/density_outer/pallas_call | solution.py:437
  118.1 13.6 %all-to-all-start.1 = ((f32[128,4,128]{2,1,0:T(4,128)}), f32[128,4,128]{2,1,0:T(4,128)S(1)}, u32[]{:S(2)}, u32[]{:S(2)}) async-start(f32[128,4,128]{2,1,0:T(4,128)} %bitcast.7), calls=%async_computation.1 | async-start | bytes 524288 | tf_op jit(solution)/shard_map/all_to_all | solution.py:491
  131.8 1.6 copy-done.22
  133.3 20.5 %density_inner.1.inner = f32[256,256]{1,0:T(8,128)S(1)} custom-call(s32[1]{0:T(128)} %bitcast.10.count, s32[640]{0:T(1024)S(1)} %concatenate.15.units, f32[257,2,8,128]{3,2,1,0:T(8,128)S(1)} %copy-done.22, bf16[48,256]{1,0:T(8,128)(2,1)S(1)} %get-tuple-element.47.pick), custom_call_target="tpu_custom_call" | custom-call | flops 10485760000 | bytes 2097152 | tf_op jit(solution)/shard_map/density_inner/pallas_call | solution.py:437
  156.5 2.4 factor.1
  160.3 11.1 %all-to-all-start.2 = ((f32[128,4,128]{2,1,0:T(4,128)}), f32[128,4,128]{2,1,0:T(4,128)S(1)}, u32[]{:S(2)}, u32[]{:S(2)}) async-start(f32[128,4,128]{2,1,0:T(4,128)} %bitcast.29), calls=%async_computation.2 | async-start | bytes 524288 | tf_op jit(solution)/shard_map/all_to_all | solution.py:491
  171.4 1.6 copy-done.23
  173.9 45.7 %force_self.1.self_acc = f32[3,256,256]{2,1,0:T(8,128)S(1)} custom-call(s32[1]{0:T(128)} %bitcast.3.count, s32[1152]{0:T(1024)S(1)} %concatenate.12.units, f32[257,2,8,128]{3,2,1,0:T(8,128)S(1)} %copy-done.23, f32[256,256]{1,0:T(8,128)S(1)} %copy-done.27, bf16[48,256]{1,0:T(8,128)(2,1)S(1)} %get-tuple-element.46.pick), custom_call_target="tpu_custom_call" | custom-call | flops 25165824000 | bytes 2097152 | tf_op jit(solution)/shard_map/force_self/pallas_call | solution.py:437
  219.7 1.6 copy-done.24
  221.3 42.1 %force_outer.1 = (f32[3,256,256]{2,1,0:T(8,128)S(1)}, f32[256,2,4,128]{3,2,1,0:T(4,128)}) custom-call(s32[1]{0:T(128)} %bitcast.6.count, s32[1152]{0:T(1024)S(1)} %concatenate.14.units, f32[257,2,8,128]{3,2,1,0:T(8,128)S(1)} %copy-done.24, f32[256,2,8,128]{3,2,1,0:T(8,128)S(1)} %bitcast.25, f32[256,256]{1,0:T(8,128)S(1)} %copy-done.27, ...), custom_call_target="tpu_custom_call" | custom-call | flops 20971520000 | bytes 2097152 | tf_op jit(solution)/shard_map/force_outer/pallas_call | solution.py:437
  264.3 13.3 %all-to-all-start.3 = ((f32[128,4,4,128]{3,2,1,0:T(4,128)}), f32[128,4,4,128]{3,2,1,0:T(4,128)S(1)}, u32[]{:S(2)}, u32[]{:S(2)}) async-start(f32[128,4,4,128]{3,2,1,0:T(4,128)} %bitcast.13), calls=%async_computation.3 | async-start | bytes 2097152 | tf_op jit(solution)/shard_map/all_to_all | solution.py:491
  277.6 1.6 copy-done.25
  279.1 19.7 %force_inner.1.inner_acc = f32[3,256,256]{2,1,0:T(8,128)S(1)} custom-call(s32[1]{0:T(128)} %bitcast.10.count, s32[640]{0:T(1024)S(1)} %concatenate.15.units, f32[257,2,8,128]{3,2,1,0:T(8,128)S(1)} %copy-done.25, f32[256,256]{1,0:T(8,128)S(1)} %copy-done.27, bf16[48,256]{1,0:T(8,128)(2,1)S(1)} %get-tuple-element.46.pick), custom_call_target="tpu_custom_call" | custom-call | flops 10485760000 | bytes 2097152 | tf_op jit(solution)/shard_map/force_inner/pallas_call | solution.py:437
  299.8 1.1 copy-done.4
  300.9 1.1 copy-done.6
  302.0 4.8 %final.1 = f32[3,256,256]{2,1,0:T(8,128)} custom-call(s32[1,256]{1,0:T(1,128)S(1)} %copy-done.18, f32[3,256,256]{2,1,0:T(8,128)S(1)} %force_self.1.self_acc, f32[3,256,256]{2,1,0:T(8,128)S(1)} %copy-done.6, f32[3,256,256]{2,1,0:T(8,128)S(1)} %copy-done.4, f32[256,2,4,128]{3,2,1,0:T(4,128)S(1)} %bitcast.22), custom_call_target="tpu_custom_call" | custom-call | bytes 2097152 | tf_op jit(solution)/shard_map/final/pallas_call | solution.py:437
  (104 shorter events, 20.6 us)
Async XLA Ops:
  0.6 1.0 copy-start.1
  1.6 1.1 copy-start.7
  2.7 0.9 copy-start.8
  7.6 1.3 copy-start
  8.9 1.4 copy-start.19
  10.3 11.5 %copy-start.16 = (s32[256]{0:T(256)S(1)}, s32[256]{0:T(256)}, u32[]{:S(2)}) copy-start(s32[256]{0:T(256)} %counts.1) | copy-start | bytes 3076
  10.3 13.1 %copy-start.28 = (s32[2,384]{1,0:T(2,128)S(1)}, s32[2,384]{1,0:T(2,128)}, u32[]{:S(2)}) copy-start(s32[2,384]{1,0:T(2,128)} %param.13) | copy-start | bytes 9220
  10.3 55.1 %all-to-all-start = ((f32[128,4,8,128]{3,2,1,0:T(8,128)}), f32[128,4,8,128]{3,2,1,0:T(8,128)S(1)}, u32[]{:S(2)}, u32[]{:S(2)}) async-start(f32[128,4,8,128]{3,2,1,0:T(8,128)} %bitcast.26), calls=%async_computation | async-start | bytes 4194304 | tf_op jit(solution)/shard_map/all_to_all | solution.py:491
  29.6 1.6 copy-start.20
  70.6 1.6 copy-start.21
  118.1 36.4 %all-to-all-start.1 = ((f32[128,4,128]{2,1,0:T(4,128)}), f32[128,4,128]{2,1,0:T(4,128)S(1)}, u32[]{:S(2)}, u32[]{:S(2)}) async-start(f32[128,4,128]{2,1,0:T(4,128)} %bitcast.7), calls=%async_computation.1 | async-start | bytes 524288 | tf_op jit(solution)/shard_map/all_to_all | solution.py:491
  131.7 1.6 copy-start.22
  133.3 21.2 %copy-start.2 = (f32[256,256]{1,0:T(8,128)S(1)}, f32[256,256]{1,0:T(8,128)}, u32[]{:S(2)}) copy-start(f32[256,256]{1,0:T(8,128)} %smooth.3) | copy-start | bytes 786436
  133.3 21.2 %copy-start.9 = (f32[256,256]{1,0:T(8,128)S(1)}, f32[256,256]{1,0:T(8,128)}, u32[]{:S(2)}) copy-start(f32[256,256]{1,0:T(8,128)} %entropy.1) | copy-start | bytes 786436
  133.3 21.2 %copy-start.18 = (s32[1,256]{1,0:T(1,128)S(1)}, s32[1,256]{1,0:T(1,128)}, u32[]{:S(2)}) copy-start(s32[1,256]{1,0:T(1,128)} %targets.3) | copy-start | bytes 3076
  154.6 1.0 copy-start.11
  155.5 0.9 copy-start.13
  160.3 59.4 %all-to-all-start.2 = ((f32[128,4,128]{2,1,0:T(4,128)}), f32[128,4,128]{2,1,0:T(4,128)S(1)}, u32[]{:S(2)}, u32[]{:S(2)}) async-start(f32[128,4,128]{2,1,0:T(4,128)} %bitcast.29), calls=%async_computation.2 | async-start | bytes 524288 | tf_op jit(solution)/shard_map/all_to_all | solution.py:491
  171.4 1.6 copy-start.23
  219.7 1.6 copy-start.24
  264.3 35.5 %all-to-all-start.3 = ((f32[128,4,4,128]{3,2,1,0:T(4,128)}), f32[128,4,4,128]{3,2,1,0:T(4,128)S(1)}, u32[]{:S(2)}, u32[]{:S(2)}) async-start(f32[128,4,4,128]{3,2,1,0:T(4,128)} %bitcast.13), calls=%async_computation.3 | async-start | bytes 2097152 | tf_op jit(solution)/shard_map/all_to_all | solution.py:491
  277.6 1.6 copy-start.25
  299.8 1.1 copy-start.4
  300.9 1.1 copy-start.6
  (9 other events, 6.9 us)

commit v5 on v4

--- a/solution.py
+++ b/solution.py
@@ -214,7 +214,7 @@
         stage_c(restore(value_slots, k), *unit(jnp.maximum(count * unroll - lag + k, 0)))
 
 
-HANDED = {"density_self": (2, 1), "density": (2, 1), "force_self": (2, 2), "force": (2, 1)}
+HANDED = {"density_self": (2, 2), "density": (1, 2), "force_self": (2, 1), "force": (1, 2)}
 
 
 def slot_shapes(kind):
@@ -495,7 +495,7 @@
     cells, tile = smooth.shape
     num_pairs = cell_pairs.shape[1]
     slots = send_cells.shape[1]
-    unroll = 32
+    unroll = 40
     targets = send_cells[0]
     padded = (cells + 1, 2, 8, LANES)
     whole = (cells + 1 + slots, 2, 8, LANES)

time: 310 us -> 303 us (0.977)
  the two profiles are of different devices: /device:TPU:1 before, /device:TPU:49 now
where the time goes in v5:
time: 303 us; the launch traced here: 300 us
  Pallas kernels  212 us (70%)
  starting transfers between devices  48.7 us (16%)
  local copies, waits for them, and re-layouts  27 us (9%)
  other arithmetic  9.18 us (3%)
  between operations  3.83 us (1%)
    pallas_call x9, Pallas kernels, launch(): pl.pallas_call(body, out_shape=[jax.ShapeDtypeStruct(shape, F32) for shap...  212 us
    all_to_all x4, starting transfers between devices, trade(): lax.all_to_all(by_peer, AXES, split_axis=0, concat_axis=0, tiled=True)  48.7 us
    unnamed x58, local copies, waits for them, and re-layouts  26.2 us
  transfers between devices with their start and end apart: 4, of which 0 were waited for; matrix products, arithmetic and copies ran while one was open for 2% of the time, Pallas kernels for 39%

profile of v5, /device:TPU:49, one launch (start us, length us, event | category | flops | bytes accessed | tf_op | source)
XLA Modules:
  0.0 300.2 jit_solution(6676881849187294221)
XLA Ops:
  1.6 1.1 copy-done.7
  5.0 2.6 prepare.1
  7.6 1.3 copy-done
  8.9 1.4 copy-done.19
  10.3 10.4 %all-to-all-start = ((f32[128,4,8,128]{3,2,1,0:T(8,128)}), f32[128,4,8,128]{3,2,1,0:T(8,128)S(1)}, u32[]{:S(2)}, u32[]{:S(2)}) async-start(f32[128,4,8,128]{3,2,1,0:T(8,128)} %bitcast.26), calls=%async_computation | async-start | bytes 4194304 | tf_op jit(solution)/shard_map/all_to_all | solution.py:491
  28.5 1.6 copy-done.20
  30.1 31.5 %density_self.1.self_rho = f32[256,256]{1,0:T(8,128)S(1)} custom-call(s32[1]{0:T(128)} %bitcast.3.count, s32[1152]{0:T(1024)S(1)} %concatenate.12.units, f32[257,2,8,128]{3,2,1,0:T(8,128)S(1)} %copy-done.20, bf16[48,256]{1,0:T(8,128)(2,1)S(1)} %get-tuple-element.47.pick), custom_call_target="tpu_custom_call" | custom-call | flops 25165824000 | bytes 2097152 | tf_op jit(solution)/shard_map/density_self/pallas_call | solution.py:437
  66.8 1.6 copy-done.21
  68.4 44.0 %density_outer.1 = (f32[256,256]{1,0:T(8,128)S(1)}, f32[256,1,256]{2,1,0:T(1,128)}) custom-call(s32[1]{0:T(128)} %bitcast.6.count, s32[1152]{0:T(1024)S(1)} %concatenate.14.units, f32[257,2,8,128]{3,2,1,0:T(8,128)S(1)} %copy-done.21, f32[256,2,8,128]{3,2,1,0:T(8,128)S(1)} %bitcast.24, bf16[48,256]{1,0:T(8,128)(2,1)S(1)} %get-tuple-element.47.pick), custom_call_target="tpu_custom_call" | custom-call | flops 20971520000 | bytes 2097152 | tf_op jit(solution)/shard_map/density_outer/pallas_call | solution.py:437
  113.1 13.8 %all-to-all-start.1 = ((f32[128,4,128]{2,1,0:T(4,128)}), f32[128,4,128]{2,1,0:T(4,128)S(1)}, u32[]{:S(2)}, u32[]{:S(2)}) async-start(f32[128,4,128]{2,1,0:T(4,128)} %bitcast.7), calls=%async_computation.1 | async-start | bytes 524288 | tf_op jit(solution)/shard_map/all_to_all | solution.py:491
  127.0 1.6 copy-done.22
  128.6 21.7 %density_inner.1.inner = f32[256,256]{1,0:T(8,128)S(1)} custom-call(s32[1]{0:T(128)} %bitcast.10.count, s32[640]{0:T(1024)S(1)} %concatenate.15.units, f32[257,2,8,128]{3,2,1,0:T(8,128)S(1)} %copy-done.22, bf16[48,256]{1,0:T(8,128)(2,1)S(1)} %get-tuple-element.47.pick), custom_call_target="tpu_custom_call" | custom-call | flops 10485760000 | bytes 2097152 | tf_op jit(solution)/shard_map/density_inner/pallas_call | solution.py:437
  152.9 2.4 factor.1
  156.8 10.3 %all-to-all-start.2 = ((f32[128,4,128]{2,1,0:T(4,128)}), f32[128,4,128]{2,1,0:T(4,128)S(1)}, u32[]{:S(2)}, u32[]{:S(2)}) async-start(f32[128,4,128]{2,1,0:T(4,128)} %bitcast.29), calls=%async_computation.2 | async-start | bytes 524288 | tf_op jit(solution)/shard_map/all_to_all | solution.py:491
  167.0 1.6 copy-done.23
  169.6 42.5 %force_self.1.self_acc = f32[3,256,256]{2,1,0:T(8,128)S(1)} custom-call(s32[1]{0:T(128)} %bitcast.3.count, s32[1152]{0:T(1024)S(1)} %concatenate.12.units, f32[257,2,8,128]{3,2,1,0:T(8,128)S(1)} %copy-done.23, f32[256,256]{1,0:T(8,128)S(1)} %copy-done.27, bf16[48,256]{1,0:T(8,128)(2,1)S(1)} %get-tuple-element.46.pick), custom_call_target="tpu_custom_call" | custom-call | flops 25165824000 | bytes 2097152 | tf_op jit(solution)/shard_map/force_self/pallas_call | solution.py:437
  212.1 1.6 copy-done.24
  213.7 41.0 %force_outer.1 = (f32[3,256,256]{2,1,0:T(8,128)S(1)}, f32[256,2,4,128]{3,2,1,0:T(4,128)}) custom-call(s32[1]{0:T(128)} %bitcast.6.count, s32[1152]{0:T(1024)S(1)} %concatenate.14.units, f32[257,2,8,128]{3,2,1,0:T(8,128)S(1)} %copy-done.24, f32[256,2,8,128]{3,2,1,0:T(8,128)S(1)} %bitcast.25, f32[256,256]{1,0:T(8,128)S(1)} %copy-done.27, ...), custom_call_target="tpu_custom_call" | custom-call | flops 20971520000 | bytes 2097152 | tf_op jit(solution)/shard_map/force_outer/pallas_call | solution.py:437
  255.6 14.1 %all-to-all-start.3 = ((f32[128,4,4,128]{3,2,1,0:T(4,128)}), f32[128,4,4,128]{3,2,1,0:T(4,128)S(1)}, u32[]{:S(2)}, u32[]{:S(2)}) async-start(f32[128,4,4,128]{3,2,1,0:T(4,128)} %bitcast.13), calls=%async_computation.3 | async-start | bytes 2097152 | tf_op jit(solution)/shard_map/all_to_all | solution.py:491
  269.7 1.6 copy-done.25
  271.3 20.9 %force_inner.1.inner_acc = f32[3,256,256]{2,1,0:T(8,128)S(1)} custom-call(s32[1]{0:T(128)} %bitcast.10.count, s32[640]{0:T(1024)S(1)} %concatenate.15.units, f32[257,2,8,128]{3,2,1,0:T(8,128)S(1)} %copy-done.25, f32[256,256]{1,0:T(8,128)S(1)} %copy-done.27, bf16[48,256]{1,0:T(8,128)(2,1)S(1)} %get-tuple-element.46.pick), custom_call_target="tpu_custom_call" | custom-call | flops 10485760000 | bytes 2097152 | tf_op jit(solution)/shard_map/force_inner/pallas_call | solution.py:437
  293.1 1.1 copy-done.4
  294.2 1.1 copy-done.6
  295.4 4.8 %final.1 = f32[3,256,256]{2,1,0:T(8,128)} custom-call(s32[1,256]{1,0:T(1,128)S(1)} %copy-done.18, f32[3,256,256]{2,1,0:T(8,128)S(1)} %force_self.1.self_acc, f32[3,256,256]{2,1,0:T(8,128)S(1)} %copy-done.6, f32[3,256,256]{2,1,0:T(8,128)S(1)} %copy-done.4, f32[256,2,4,128]{3,2,1,0:T(4,128)S(1)} %bitcast.22), custom_call_target="tpu_custom_call" | custom-call | bytes 2097152 | tf_op jit(solution)/shard_map/final/pallas_call | solution.py:437
  (104 shorter events, 20.6 us)
Async XLA Ops:
  0.6 1.0 copy-start.1
  1.6 1.1 copy-start.7
  2.7 0.9 copy-start.8
  7.6 1.3 copy-start
  8.9 1.4 copy-start.19
  10.3 10.5 %copy-start.16 = (s32[256]{0:T(256)S(1)}, s32[256]{0:T(256)}, u32[]{:S(2)}) copy-start(s32[256]{0:T(256)} %counts.1) | copy-start | bytes 3076
  10.3 12.1 %copy-start.28 = (s32[2,384]{1,0:T(2,128)S(1)}, s32[2,384]{1,0:T(2,128)}, u32[]{:S(2)}) copy-start(s32[2,384]{1,0:T(2,128)} %param.13) | copy-start | bytes 9220
  10.3 51.3 %all-to-all-start = ((f32[128,4,8,128]{3,2,1,0:T(8,128)}), f32[128,4,8,128]{3,2,1,0:T(8,128)S(1)}, u32[]{:S(2)}, u32[]{:S(2)}) async-start(f32[128,4,8,128]{3,2,1,0:T(8,128)} %bitcast.26), calls=%async_computation | async-start | bytes 4194304 | tf_op jit(solution)/shard_map/all_to_all | solution.py:491
  28.5 1.6 copy-start.20
  66.8 1.6 copy-start.21
  113.1 37.9 %all-to-all-start.1 = ((f32[128,4,128]{2,1,0:T(4,128)}), f32[128,4,128]{2,1,0:T(4,128)S(1)}, u32[]{:S(2)}, u32[]{:S(2)}) async-start(f32[128,4,128]{2,1,0:T(4,128)} %bitcast.7), calls=%async_computation.1 | async-start | bytes 524288 | tf_op jit(solution)/shard_map/all_to_all | solution.py:491
  127.0 1.6 copy-start.22
  128.6 22.5 %copy-start.2 = (f32[256,256]{1,0:T(8,128)S(1)}, f32[256,256]{1,0:T(8,128)}, u32[]{:S(2)}) copy-start(f32[256,256]{1,0:T(8,128)} %smooth.3) | copy-start | bytes 786436
  128.6 22.5 %copy-start.9 = (f32[256,256]{1,0:T(8,128)S(1)}, f32[256,256]{1,0:T(8,128)}, u32[]{:S(2)}) copy-start(f32[256,256]{1,0:T(8,128)} %entropy.1) | copy-start | bytes 786436
  128.6 22.5 %copy-start.18 = (s32[1,256]{1,0:T(1,128)S(1)}, s32[1,256]{1,0:T(1,128)}, u32[]{:S(2)}) copy-start(s32[1,256]{1,0:T(1,128)} %targets.3) | copy-start | bytes 3076
  151.0 1.0 copy-start.11
  152.0 0.9 copy-start.13
  156.8 55.4 %all-to-all-start.2 = ((f32[128,4,128]{2,1,0:T(4,128)}), f32[128,4,128]{2,1,0:T(4,128)S(1)}, u32[]{:S(2)}, u32[]{:S(2)}) async-start(f32[128,4,128]{2,1,0:T(4,128)} %bitcast.29), calls=%async_computation.2 | async-start | bytes 524288 | tf_op jit(solution)/shard_map/all_to_all | solution.py:491
  167.0 1.6 copy-start.23
  212.1 1.6 copy-start.24
  255.6 37.5 %all-to-all-start.3 = ((f32[128,4,4,128]{3,2,1,0:T(4,128)}), f32[128,4,4,128]{3,2,1,0:T(4,128)S(1)}, u32[]{:S(2)}, u32[]{:S(2)}) async-start(f32[128,4,4,128]{3,2,1,0:T(4,128)} %bitcast.13), calls=%async_computation.3 | async-start | bytes 2097152 | tf_op jit(solution)/shard_map/all_to_all | solution.py:491
  269.7 1.6 copy-start.25
  293.1 1.1 copy-start.4
  294.2 1.1 copy-start.6
  (9 other events, 6.9 us)
